TPU v7x, 32 devices: a whole 2x2x4 slice. The times are simulated.
32 devices in a mesh: ctx: 8 (over z, y), head: 4 (over x, core).
Axes of the slice: x: 2, y: 2, z: 4, core: 2. Of those that a mesh axis runs over, the one named last changes fastest.
Arguments:
- queries: bfloat16 [4096, 4096], P('ctx', 'head'), may hold values from -8 to 8
- keys: bfloat16 [4096, 1024], P('ctx', 'head'), may hold values from -8 to 8
- values: bfloat16 [4096, 1024], P('ctx', 'head'), may hold values from -6 to 6
- output_gradient: bfloat16 [4096, 4096], P('ctx', 'head'), may hold values from -6 to 6
- blocks: int32 [32, 8], P('ctx'), may hold values from 0 to 31, as said below
- counts: int32 [32], P('ctx'), may hold values from 2 to 8, as said below
Outputs:
- dqueries: bfloat16 [4096, 4096], P(('ctx', 'head'))
- dkeys: bfloat16 [4096, 1024], P(('ctx', 'head'))
- dvalues: bfloat16 [4096, 1024], P(('ctx', 'head'))
Inputs may be any that keep to these rules, and one draw needn't show every extreme that they name: For the query block b on token shard i = b // 4, all 8 entries of row b are distinct and name key blocks of the shards i - 2 to i + 2, taken around the closed cycle of 32 blocks. `counts`: some rows have all 8 entries live.
All inputs are finite; a program needn't handle non-finite values.
Results may differ from a plain program's by a relative error of at most 0.0088.
Values may be sent and summed in bfloat16 or wider, within the bound.
No kernel may reach another device: no remote copies, remote signals or barrier semaphores. Data moves between devices by JAX's collectives and lax.ppermute only.
A program may use at most 64 MiB of HBM per device.

v0:
```python
import math

import jax
import jax.numpy as jnp
from jax import lax
from jax.sharding import PartitionSpec as P

HEAD_SIZE = 128
BLOCK_TOKENS = 128
SLOTS = 8
REACH = 2


def from_behind(x, axis, by):
    size = lax.axis_size(axis)
    return lax.ppermute(x, axis, [(i, (i + by) % size) for i in range(size)])


def send_back(segment, shift_by):
    return from_behind(segment, "ctx", shift_by)


def kv_neighbour(piece, offset):
    return from_behind(piece, "ctx", -offset)


def collect_window(piece, axis_dim, fetcher):
    pieces = []
    for offset in range(-REACH, REACH + 1):
        if offset == 0:
            pieces.append(piece)
        else:
            pieces.append(fetcher(piece, offset))
    return jnp.concatenate(pieces, axis=axis_dim)


def on_device(queries, keys, values, output_gradient, blocks, counts):
    tok_rows, query_width = queries.shape
    kv_width = keys.shape[1]
    kv_heads = kv_width // HEAD_SIZE
    query_group = query_width // kv_width
    own_blocks = tok_rows // BLOCK_TOKENS
    cycle_size = lax.axis_size("ctx")
    my_index = lax.axis_index("ctx")
    softmax_scale = 1.0 / math.sqrt(HEAD_SIZE)
    stacked = jnp.stack([keys, values])
    extended = collect_window(stacked, 1, kv_neighbour)
    window_blocks = (2 * REACH + 1) * own_blocks
    extended = extended.reshape(2, window_blocks, BLOCK_TOKENS, kv_heads, HEAD_SIZE)
    first_block = (my_index - REACH) * own_blocks
    local_blocks = jnp.mod(blocks - first_block, cycle_size * own_blocks)
    blocked_queries = queries.reshape(own_blocks, BLOCK_TOKENS, kv_heads, query_group, HEAD_SIZE)
    output_blocks = output_gradient.reshape(
        own_blocks, BLOCK_TOKENS, kv_heads, query_group, HEAD_SIZE
    )

    def one_block(qblock, running):
        gradients, dquery_blocks, stat_blocks = running
        slot_blocks = local_blocks[qblock]
        live_slots = jnp.arange(SLOTS) < counts[qblock]
        live_mask = live_slots[None, None, None, :, None]
        kblock = extended[0][slot_blocks]
        vblock = extended[1][slot_blocks]
        qrows = blocked_queries[qblock]
        orows = output_blocks[qblock]
        scores = (
            jnp.einsum("rhgd,schd->hgrsc", qrows, kblock, preferred_element_type=jnp.float32)
            * softmax_scale
        )
        scores = jnp.where(live_mask, scores, -1e30)
        row_max = jnp.max(scores, axis=(3, 4), keepdims=True)
        weights = jnp.where(live_mask, jnp.exp(scores - row_max), 0.0)
        total = jnp.sum(weights, axis=(3, 4), keepdims=True)
        probs = weights / total
        dprobs = jnp.einsum("rhgd,schd->hgrsc", orows, vblock, preferred_element_type=jnp.float32)
        row_delta = jnp.sum(probs * dprobs, axis=(3, 4), keepdims=True)
        dscores = (probs * (dprobs - row_delta)).astype(jnp.bfloat16)
        dquery = softmax_scale * jnp.einsum(
            "hgrsc,schd->rhgd", dscores, kblock, preferred_element_type=jnp.float32
        )
        dquery_blocks = dquery_blocks.at[qblock].set(dquery.astype(jnp.bfloat16))
        probs_bf = probs.astype(jnp.bfloat16)
        dkey_part = softmax_scale * jnp.einsum(
            "hgrsc,rhgd->schd", dscores, qrows, preferred_element_type=jnp.float32
        )
        dvalue_part = jnp.einsum(
            "hgrsc,rhgd->schd", probs_bf, orows, preferred_element_type=jnp.float32
        )
        gradients = gradients.at[0, slot_blocks].add(dkey_part)
        gradients = gradients.at[1, slot_blocks].add(dvalue_part)
        return (gradients, dquery_blocks, stat_blocks)

    start_grads = jnp.zeros((2, window_blocks, BLOCK_TOKENS, kv_heads, HEAD_SIZE), jnp.float32)
    start_dquery = jnp.zeros(
        (own_blocks, BLOCK_TOKENS, kv_heads, query_group, HEAD_SIZE), jnp.bfloat16
    )
    start_stats = jnp.zeros((2, own_blocks, BLOCK_TOKENS, kv_heads, query_group), jnp.float32)
    gradients, dquery_blocks, stat_blocks = lax.fori_loop(
        0, own_blocks, one_block, (start_grads, start_dquery, start_stats)
    )
    segments = gradients.reshape(2, 2 * REACH + 1, tok_rows, kv_width)
    summed = segments[:, REACH]
    for offset in range(1, REACH + 1):
        for direction in (1, -1):
            summed = summed + send_back(segments[:, REACH + direction * offset], direction * offset)
    dkeys = summed[0].astype(jnp.bfloat16)
    dvalues = summed[1].astype(jnp.bfloat16)
    dqueries = dquery_blocks.reshape(tok_rows, query_width)
    return (
        lax.all_to_all(dqueries, "head", split_axis=0, concat_axis=1, tiled=True),
        lax.all_to_all(dkeys, "head", split_axis=0, concat_axis=1, tiled=True),
        lax.all_to_all(dvalues, "head", split_axis=0, concat_axis=1, tiled=True),
    )


def solution(mesh):
    return jax.shard_map(
        on_device,
        mesh=mesh,
        in_specs=(
            P("ctx", "head"),
            P("ctx", "head"),
            P("ctx", "head"),
            P("ctx", "head"),
            P("ctx", None),
            P("ctx"),
        ),
        out_specs=(P(("ctx", "head"), None), P(("ctx", "head"), None), P(("ctx", "head"), None)),
        check_vma=False,
    )
```

profile of v0, /device:TPU:0, one launch (start us, length us, event | category | flops | bytes accessed | tf_op | source)
XLA Modules:
  0.0 317.5 jit_solution(17692302766995053355)
XLA Ops:
  0.7 1.9 pad_maximum_fusion
  2.6 3.0 collective-permute-start
  7.1 3.2 %collective-permute-start.2 = (bf16[2,512,256]{2,1,0:T(8,128)(2,1)}, bf16[2,512,256]{2,1,0:T(8,128)(2,1)}, u32[]{:S(2)}, u32[]{:S(2)}) collective-permute-start(bf16[2,512,256]{2,1,0:T(8,128)(2,1)} %pad_maximum_fusion), channel_id=1, source_target_pairs={{0,28},{4,0},{8,4},{12,8},{16,12},{20,16},{24,20},{28,24},{1,29},{... | collective-permute-start | bytes 1572872 | tf_op jit(solution)/shard_map/ppermute | solution.py:16
  11.3 2.6 reshape.148
  13.9 2.6 reshape.150
  16.5 4.3 %collective-permute-done = bf16[2,512,256]{2,1,0:T(8,128)(2,1)} collective-permute-done((bf16[2,512,256]{2,1,0:T(8,128)(2,1)}, bf16[2,512,256]{2,1,0:T(8,128)(2,1)}, u32[]{:S(2)}, u32[]{:S(2)}) %collective-permute-start) | collective-permute-done | bytes 524320 | tf_op jit(solution)/shard_map/ppermute | solution.py:16
  21.8 11.4 %collective-permute-done.1 = bf16[2,512,256]{2,1,0:T(8,128)(2,1)} collective-permute-done((bf16[2,512,256]{2,1,0:T(8,128)(2,1)}, bf16[2,512,256]{2,1,0:T(8,128)(2,1)}, u32[]{:S(2)}, u32[]{:S(2)}) %collective-permute-start.1) | collective-permute-done | bytes 524320 | tf_op jit(solution)/shard_map/ppermute | solution.py:16
  35.4 6.9 %collective-permute-done.3 = bf16[2,512,256]{2,1,0:T(8,128)(2,1)} collective-permute-done((bf16[2,512,256]{2,1,0:T(8,128)(2,1)}, bf16[2,512,256]{2,1,0:T(8,128)(2,1)}, u32[]{:S(2)}, u32[]{:S(2)}) %collective-permute-start.3) | collective-permute-done | bytes 524320 | tf_op jit(solution)/shard_map/ppermute | solution.py:16
  43.4 2.8 reshape.149
  46.2 2.9 broadcast_in_dim.65
  50.4 151.3 %while.16 = (s32[]{:T(128)}, f32[2,20,128,2,128]{4,2,3,1,0:T(8,128)}, bf16[4,128,2,4,128]{1,4,3,2,0:T(8,128)(2,1)}, s32[4,8]{1,0:T(4,128)S(1)}, bf16[4,128,2,4,1...) while((s32[]{:T(128)}, ...), condition=%wide.region_7.8_spmd, body=%wide.region_0.7_spmd.sunk | while | flops 1373763712 | bytes 96519896 | solution.py:98
  50.4 4.0 %slice_bitcast_fusion.8 = (bf16[20,128,2,128]{3,2,1,0:T(2,128)(2,1)S(1)}, bf16[20,128,2,128]{3,2,1,0:T(2,128)(2,1)S(1)}) fusion(bf16[2,20,128,2,128]{4,3,2,1,0:T(2,128)(2,1)} %get-tuple-element.337), kind=kLoop, calls=%fused_computation.25.clone.1 | loop fusion | bytes 5242880 | tf_op jit(solution)/shard_map/while/body/eval_jaxpr/squeeze | solution.py:62
  54.4 1.6 gather_fusion
  62.2 2.4 fusion.67
  66.1 1.6 gather_fusion.1
  67.7 3.8 %fusion.64 = (f32[2,4,128]{2,1,0:T(4,128)S(1)}, f32[2,8,128,128,4]{3,2,4,1,0:T(8,128)S(1)}) fusion(f32[2,4,128]{2,1,0:T(4,128)S(1)} %fusion.63, f32[2,4,128]{2,1,0:T(4,128)S(1)} %get-tuple-element.303, f32[2,8,128,128,4]{3,2,4,1,0:T(8,128)} %copy-done, pred[8]{0:T(512)(128)(4,1)S(1)} %iota_compare_fusion.2, ...), kind=kOutput, calls=%fused_computation.6.clone.1 | convolution fusion | flops 275774464 | bytes 9187336 | tf_op jit(solution)/shard_map/while/body/eval_jaxpr/rhgd,schd->hgrsc/dot_general | solution.py:75
  73.0 1.8 fusion.66
  74.8 2.6 copy.185
  77.4 3.8 %scatter_fusion = f32[2,20,128,2,128]{4,2,3,1,0:T(8,128)} fusion(f32[2,20,128,2,128]{4,2,3,1,0:T(8,128)} %get-tuple-element.321, s32[8]{0:T(128)S(1)} %select_bitcast_fusion.5, f32[8,128,2,128]{3,1,2,0:T(8,128)} %copy.185), kind=kCustom, calls=%fused_computation.2.clone.1 | custom fusion | flops 262144 | bytes 3145792 | tf_op jit(solution)/shard_map/while/body/eval_jaxpr/scatter-add | solution.py:89
  81.1 3.4 %scatter_fusion.1 = f32[2,20,128,2,128]{4,2,3,1,0:T(8,128)} fusion(f32[2,20,128,2,128]{4,2,3,1,0:T(8,128)} %scatter_fusion, s32[8]{0:T(128)S(1)} %get-tuple-element.308, f32[8,128,2,128]{3,1,2,0:T(8,128)S(1)} %copy.186), kind=kCustom, calls=%fused_computation.3.clone.1 | custom fusion | flops 262144 | bytes 3145792 | tf_op jit(solution)/shard_map/while/body/eval_jaxpr/scatter-add | solution.py:90
  85.2 2.9 fusion.68
  88.2 4.0 %slice_bitcast_fusion.8 = (bf16[20,128,2,128]{3,2,1,0:T(2,128)(2,1)S(1)}, bf16[20,128,2,128]{3,2,1,0:T(2,128)(2,1)S(1)}) fusion(bf16[2,20,128,2,128]{4,3,2,1,0:T(2,128)(2,1)} %get-tuple-element.337), kind=kLoop, calls=%fused_computation.25.clone.1 | loop fusion | bytes 5242880 | tf_op jit(solution)/shard_map/while/body/eval_jaxpr/squeeze | solution.py:62
  92.2 1.6 gather_fusion
  100.0 2.4 fusion.67
  103.9 1.6 gather_fusion.1
  105.5 3.8 %fusion.64 = (f32[2,4,128]{2,1,0:T(4,128)S(1)}, f32[2,8,128,128,4]{3,2,4,1,0:T(8,128)S(1)}) fusion(f32[2,4,128]{2,1,0:T(4,128)S(1)} %fusion.63, f32[2,4,128]{2,1,0:T(4,128)S(1)} %get-tuple-element.303, f32[2,8,128,128,4]{3,2,4,1,0:T(8,128)} %copy-done, pred[8]{0:T(512)(128)(4,1)S(1)} %iota_compare_fusion.2, ...), kind=kOutput, calls=%fused_computation.6.clone.1 | convolution fusion | flops 275774464 | bytes 9187336 | tf_op jit(solution)/shard_map/while/body/eval_jaxpr/rhgd,schd->hgrsc/dot_general | solution.py:75
  110.8 1.8 fusion.66
  112.6 2.6 copy.185
  115.2 3.7 %scatter_fusion = f32[2,20,128,2,128]{4,2,3,1,0:T(8,128)} fusion(f32[2,20,128,2,128]{4,2,3,1,0:T(8,128)} %get-tuple-element.321, s32[8]{0:T(128)S(1)} %select_bitcast_fusion.5, f32[8,128,2,128]{3,1,2,0:T(8,128)} %copy.185), kind=kCustom, calls=%fused_computation.2.clone.1 | custom fusion | flops 262144 | bytes 3145792 | tf_op jit(solution)/shard_map/while/body/eval_jaxpr/scatter-add | solution.py:89
  118.9 3.4 %scatter_fusion.1 = f32[2,20,128,2,128]{4,2,3,1,0:T(8,128)} fusion(f32[2,20,128,2,128]{4,2,3,1,0:T(8,128)} %scatter_fusion, s32[8]{0:T(128)S(1)} %get-tuple-element.308, f32[8,128,2,128]{3,1,2,0:T(8,128)S(1)} %copy.186), kind=kCustom, calls=%fused_computation.3.clone.1 | custom fusion | flops 262144 | bytes 3145792 | tf_op jit(solution)/shard_map/while/body/eval_jaxpr/scatter-add | solution.py:90
  123.0 2.9 fusion.68
  126.0 4.0 %slice_bitcast_fusion.8 = (bf16[20,128,2,128]{3,2,1,0:T(2,128)(2,1)S(1)}, bf16[20,128,2,128]{3,2,1,0:T(2,128)(2,1)S(1)}) fusion(bf16[2,20,128,2,128]{4,3,2,1,0:T(2,128)(2,1)} %get-tuple-element.337), kind=kLoop, calls=%fused_computation.25.clone.1 | loop fusion | bytes 5242880 | tf_op jit(solution)/shard_map/while/body/eval_jaxpr/squeeze | solution.py:62
  130.0 1.6 gather_fusion
  137.8 2.4 fusion.67
  141.7 1.6 gather_fusion.1
  143.3 3.8 %fusion.64 = (f32[2,4,128]{2,1,0:T(4,128)S(1)}, f32[2,8,128,128,4]{3,2,4,1,0:T(8,128)S(1)}) fusion(f32[2,4,128]{2,1,0:T(4,128)S(1)} %fusion.63, f32[2,4,128]{2,1,0:T(4,128)S(1)} %get-tuple-element.303, f32[2,8,128,128,4]{3,2,4,1,0:T(8,128)} %copy-done, pred[8]{0:T(512)(128)(4,1)S(1)} %iota_compare_fusion.2, ...), kind=kOutput, calls=%fused_computation.6.clone.1 | convolution fusion | flops 275774464 | bytes 9187336 | tf_op jit(solution)/shard_map/while/body/eval_jaxpr/rhgd,schd->hgrsc/dot_general | solution.py:75
  148.6 1.8 fusion.66
  150.4 2.6 copy.185
  153.0 3.8 %scatter_fusion = f32[2,20,128,2,128]{4,2,3,1,0:T(8,128)} fusion(f32[2,20,128,2,128]{4,2,3,1,0:T(8,128)} %get-tuple-element.321, s32[8]{0:T(128)S(1)} %select_bitcast_fusion.5, f32[8,128,2,128]{3,1,2,0:T(8,128)} %copy.185), kind=kCustom, calls=%fused_computation.2.clone.1 | custom fusion | flops 262144 | bytes 3145792 | tf_op jit(solution)/shard_map/while/body/eval_jaxpr/scatter-add | solution.py:89
  156.8 3.4 %scatter_fusion.1 = f32[2,20,128,2,128]{4,2,3,1,0:T(8,128)} fusion(f32[2,20,128,2,128]{4,2,3,1,0:T(8,128)} %scatter_fusion, s32[8]{0:T(128)S(1)} %get-tuple-element.308, f32[8,128,2,128]{3,1,2,0:T(8,128)S(1)} %copy.186), kind=kCustom, calls=%fused_computation.3.clone.1 | custom fusion | flops 262144 | bytes 3145792 | tf_op jit(solution)/shard_map/while/body/eval_jaxpr/scatter-add | solution.py:90
  160.9 2.9 fusion.68
  163.8 4.0 %slice_bitcast_fusion.8 = (bf16[20,128,2,128]{3,2,1,0:T(2,128)(2,1)S(1)}, bf16[20,128,2,128]{3,2,1,0:T(2,128)(2,1)S(1)}) fusion(bf16[2,20,128,2,128]{4,3,2,1,0:T(2,128)(2,1)} %get-tuple-element.337), kind=kLoop, calls=%fused_computation.25.clone.1 | loop fusion | bytes 5242880 | tf_op jit(solution)/shard_map/while/body/eval_jaxpr/squeeze | solution.py:62
  167.9 1.6 gather_fusion
  175.6 2.4 fusion.67
  181.2 3.8 %fusion.64 = (f32[2,4,128]{2,1,0:T(4,128)S(1)}, f32[2,8,128,128,4]{3,2,4,1,0:T(8,128)S(1)}) fusion(f32[2,4,128]{2,1,0:T(4,128)S(1)} %fusion.63, f32[2,4,128]{2,1,0:T(4,128)S(1)} %get-tuple-element.303, f32[2,8,128,128,4]{3,2,4,1,0:T(8,128)} %copy-done, pred[8]{0:T(512)(128)(4,1)S(1)} %iota_compare_fusion.2, ...), kind=kOutput, calls=%fused_computation.6.clone.1 | convolution fusion | flops 275774464 | bytes 9187336 | tf_op jit(solution)/shard_map/while/body/eval_jaxpr/rhgd,schd->hgrsc/dot_general | solution.py:75
  186.4 1.8 fusion.66
  188.2 2.6 copy.185
  190.8 3.8 %scatter_fusion = f32[2,20,128,2,128]{4,2,3,1,0:T(8,128)} fusion(f32[2,20,128,2,128]{4,2,3,1,0:T(8,128)} %get-tuple-element.321, s32[8]{0:T(128)S(1)} %select_bitcast_fusion.5, f32[8,128,2,128]{3,1,2,0:T(8,128)} %copy.185), kind=kCustom, calls=%fused_computation.2.clone.1 | custom fusion | flops 262144 | bytes 3145792 | tf_op jit(solution)/shard_map/while/body/eval_jaxpr/scatter-add | solution.py:89
  194.6 3.4 %scatter_fusion.1 = f32[2,20,128,2,128]{4,2,3,1,0:T(8,128)} fusion(f32[2,20,128,2,128]{4,2,3,1,0:T(8,128)} %scatter_fusion, s32[8]{0:T(128)S(1)} %get-tuple-element.308, f32[8,128,2,128]{3,1,2,0:T(8,128)S(1)} %copy.186), kind=kCustom, calls=%fused_computation.3.clone.1 | custom fusion | flops 262144 | bytes 3145792 | tf_op jit(solution)/shard_map/while/body/eval_jaxpr/scatter-add | solution.py:90
  198.7 2.9 fusion.68
  201.6 9.3 %copy.100 = f32[2,20,128,2,128]{4,3,2,1,0:T(2,128)} copy(f32[2,20,128,2,128]{4,2,3,1,0:T(8,128)} %get-tuple-element.166) | data formatting | bytes 10485760 | tf_op jit(solution)/shard_map/while | solution.py:98
  210.9 7.9 %reshape.151 = f32[2,5,512,256]{3,2,1,0:T(8,128)} reshape(f32[2,20,128,2,128]{4,3,2,1,0:T(2,128)} %copy.100) | data formatting | bytes 10485760 | tf_op jit(solution)/shard_map/reshape | solution.py:101
  218.8 4.4 %slice_bitcast_fusion.5 = (f32[2,512,256]{2,1,0:T(8,128)}, f32[2,512,256]{2,1,0:T(8,128)}, f32[2,512,256]{2,1,0:T(8,128)}, f32[2,512,256]{2,1,0:T(8,128)}) fusion(f32[2,5,512,256]{3,2,1,0:T(8,128)} %reshape.151), kind=kLoop, calls=%fused_computation.53 | loop fusion | bytes 8388608 | tf_op jit(solution)/shard_map/squeeze | solution.py:105
  224.7 3.2 %collective-permute-start.5 = (f32[2,512,256]{2,1,0:T(8,128)}, f32[2,512,256]{2,1,0:T(8,128)S(1)}, u32[]{:S(2)}, u32[]{:S(2)}) collective-permute-start(f32[2,512,256]{2,1,0:T(8,128)} %get-tuple-element.235), channel_id=1, source_target_pairs={{0,28},{4,0},{8,4},{12,8},{16,12},{20,16},{24,20},{28,24},{1,29},{... | collective-permute-start | bytes 3145736 | tf_op jit(solution)/shard_map/ppermute | solution.py:16
  228.0 3.8 %collective-permute-start.7 = (f32[2,512,256]{2,1,0:T(8,128)}, f32[2,512,256]{2,1,0:T(8,128)}, u32[]{:S(2)}, u32[]{:S(2)}) collective-permute-start(f32[2,512,256]{2,1,0:T(8,128)} %get-tuple-element.236), channel_id=1, source_target_pairs={{0,24},{4,28},{8,0},{12,4},{16,8},{20,12},{24,16},{28,20},{1,25},{... | collective-permute-start | bytes 3145736 | tf_op jit(solution)/shard_map/ppermute | solution.py:16
  233.1 3.5 %all-to-all-start = ((bf16[4,128,1024]{2,1,0:T(8,128)(2,1)}), bf16[4,128,1024]{2,1,0:T(8,128)(2,1)S(1)}, u32[]{:S(2)}, u32[]{:S(2)}) async-start(bf16[4,128,1024]{2,1,0:T(8,128)(2,1)} %copy.134), calls=%async_computation | async-start | bytes 2097152 | tf_op jit(solution)/shard_map/all_to_all | solution.py:110
  236.6 33.5 %collective-permute-done.4 = f32[2,512,256]{2,1,0:T(8,128)S(1)} collective-permute-done((f32[2,512,256]{2,1,0:T(8,128)}, f32[2,512,256]{2,1,0:T(8,128)S(1)}, u32[]{:S(2)}, u32[]{:S(2)}) %collective-permute-start.4) | collective-permute-done | bytes 1048608 | tf_op jit(solution)/shard_map/ppermute | solution.py:16
  270.1 2.1 collective-permute-done.5
  272.2 5.9 %collective-permute-done.6 = f32[2,512,256]{2,1,0:T(8,128)} collective-permute-done((f32[2,512,256]{2,1,0:T(8,128)}, f32[2,512,256]{2,1,0:T(8,128)}, u32[]{:S(2)}, u32[]{:S(2)}) %collective-permute-start.6) | collective-permute-done | bytes 1048608 | tf_op jit(solution)/shard_map/ppermute | solution.py:16
  278.1 17.5 %collective-permute-done.7 = f32[2,512,256]{2,1,0:T(8,128)} collective-permute-done((f32[2,512,256]{2,1,0:T(8,128)}, f32[2,512,256]{2,1,0:T(8,128)}, u32[]{:S(2)}, u32[]{:S(2)}) %collective-permute-start.7) | collective-permute-done | bytes 1048608 | tf_op jit(solution)/shard_map/ppermute | solution.py:16
  295.6 2.1 fusion.44
  298.5 8.6 %all_to_all.51 = bf16[4,128,256]{2,1,0:T(8,128)(2,1)S(1)} all-to-all(bf16[4,128,256]{2,1,0:T(8,128)(2,1)S(1)} %bitcast.216), channel_id=1, replica_groups=mesh['ctx'=8,'head'=4] {'head'}, dimensions={0} | all-to-all | bytes 524288 | tf_op jit(solution)/shard_map/all_to_all | solution.py:111
  307.0 3.4 %all-to-all-start.2 = ((bf16[4,128,256]{2,1,0:T(8,128)(2,1)}), bf16[4,128,256]{2,1,0:T(8,128)(2,1)S(1)}, u32[]{:S(2)}, u32[]{:S(2)}) async-start(bf16[4,128,256]{2,1,0:T(8,128)(2,1)} %bitcast.44), calls=%async_computation.2 | async-start | bytes 524288 | tf_op jit(solution)/shard_map/all_to_all | solution.py:112
  313.5 3.0 all-to-all-done.2
  (108 shorter events, 56.6 us)
Async XLA Ops:
  0.6 33.6 %copy-start.5 = (bf16[512,256]{1,0:T(8,128)(2,1)S(1)}, bf16[512,256]{1,0:T(8,128)(2,1)}, u32[]{:S(2)}) copy-start(bf16[512,256]{1,0:T(8,128)(2,1)} %param.11) | copy-start | bytes 786436
  0.6 33.6 %copy-start.4 = (bf16[512,256]{1,0:T(8,128)(2,1)S(1)}, bf16[512,256]{1,0:T(8,128)(2,1)}, u32[]{:S(2)}) copy-start(bf16[512,256]{1,0:T(8,128)(2,1)} %param.12) | copy-start | bytes 786436
  2.6 18.2 %collective-permute-start = (bf16[2,512,256]{2,1,0:T(8,128)(2,1)}, bf16[2,512,256]{2,1,0:T(8,128)(2,1)}, u32[]{:S(2)}, u32[]{:S(2)}) collective-permute-start(bf16[2,512,256]{2,1,0:T(8,128)(2,1)} %pad_maximum_fusion), channel_id=1, source_target_pairs={{0,8},{4,12},{8,16},{12,20},{16,24},{20,28},{24,0},{28,4},{1,9},{5... | collective-permute-start | bytes 1572872 | tf_op jit(solution)/shard_map/ppermute | solution.py:16
  5.6 27.6 %collective-permute-start.1 = (bf16[2,512,256]{2,1,0:T(8,128)(2,1)}, bf16[2,512,256]{2,1,0:T(8,128)(2,1)}, u32[]{:S(2)}, u32[]{:S(2)}) collective-permute-start(bf16[2,512,256]{2,1,0:T(8,128)(2,1)} %pad_maximum_fusion), channel_id=1, source_target_pairs={{0,4},{4,8},{8,12},{12,16},{16,20},{20,24},{24,28},{28,0},{1,5},{5... | collective-permute-start | bytes 1572872 | tf_op jit(solution)/shard_map/ppermute | solution.py:16
  7.1 27.2 %collective-permute-start.2 = (bf16[2,512,256]{2,1,0:T(8,128)(2,1)}, bf16[2,512,256]{2,1,0:T(8,128)(2,1)}, u32[]{:S(2)}, u32[]{:S(2)}) collective-permute-start(bf16[2,512,256]{2,1,0:T(8,128)(2,1)} %pad_maximum_fusion), channel_id=1, source_target_pairs={{0,28},{4,0},{8,4},{12,8},{16,12},{20,16},{24,20},{28,24},{1,29},{... | collective-permute-start | bytes 1572872 | tf_op jit(solution)/shard_map/ppermute | solution.py:16
  10.3 32.0 %collective-permute-start.3 = (bf16[2,512,256]{2,1,0:T(8,128)(2,1)}, bf16[2,512,256]{2,1,0:T(8,128)(2,1)}, u32[]{:S(2)}, u32[]{:S(2)}) collective-permute-start(bf16[2,512,256]{2,1,0:T(8,128)(2,1)} %pad_maximum_fusion), channel_id=1, source_target_pairs={{0,24},{4,28},{8,0},{12,4},{16,8},{20,12},{24,16},{28,20},{1,25},{... | collective-permute-start | bytes 1572872 | tf_op jit(solution)/shard_map/ppermute | solution.py:16
  46.2 4.2 %copy-start.6 = (s32[4]{0:T(128)S(1)}, s32[4]{0:T(128)}, u32[]{:S(2)}) copy-start(s32[4]{0:T(128)} %param.15) | copy-start | bytes 52
  46.2 4.2 %copy-start.7 = (s32[5]{0:T(128)S(1)}, s32[5]{0:T(128)}, u32[]{:S(2)}) copy-start(s32[5]{0:T(128)} %constant.119.clone.1) | copy-start | bytes 64
  56.5 4.6 %copy-start.2 = (bf16[8,128,2,128,1]{1,3,0,4,2:T(8,128)(2,1)}, bf16[8,128,2,128,1]{1,3,0,4,2:T(8,128)(2,1)S(1)}, u32[]{:S(2)}) copy-start(bf16[8,128,2,128,1]{1,3,0,4,2:T(8,128)(2,1)S(1)} %copy.184) | copy-start | bytes 1572868 | tf_op jit(solution)/shard_map/while
  60.1 2.0 copy-start
  67.7 3.8 %copy-start.1 = (f32[2,8,128,128,4]{3,2,4,1,0:T(8,128)S(1)}, f32[2,8,128,128,4]{3,2,4,1,0:T(8,128)}, u32[]{:S(2)}) copy-start(f32[2,8,128,128,4]{3,2,4,1,0:T(8,128)} %copy-done) | copy-start | bytes 12582916 | tf_op jit(solution)/shard_map/while
  94.3 4.6 %copy-start.2 = (bf16[8,128,2,128,1]{1,3,0,4,2:T(8,128)(2,1)}, bf16[8,128,2,128,1]{1,3,0,4,2:T(8,128)(2,1)S(1)}, u32[]{:S(2)}) copy-start(bf16[8,128,2,128,1]{1,3,0,4,2:T(8,128)(2,1)S(1)} %copy.184) | copy-start | bytes 1572868 | tf_op jit(solution)/shard_map/while
  97.9 2.0 copy-start
  105.5 3.8 %copy-start.1 = (f32[2,8,128,128,4]{3,2,4,1,0:T(8,128)S(1)}, f32[2,8,128,128,4]{3,2,4,1,0:T(8,128)}, u32[]{:S(2)}) copy-start(f32[2,8,128,128,4]{3,2,4,1,0:T(8,128)} %copy-done) | copy-start | bytes 12582916 | tf_op jit(solution)/shard_map/while
  132.1 4.6 %copy-start.2 = (bf16[8,128,2,128,1]{1,3,0,4,2:T(8,128)(2,1)}, bf16[8,128,2,128,1]{1,3,0,4,2:T(8,128)(2,1)S(1)}, u32[]{:S(2)}) copy-start(bf16[8,128,2,128,1]{1,3,0,4,2:T(8,128)(2,1)S(1)} %copy.184) | copy-start | bytes 1572868 | tf_op jit(solution)/shard_map/while
  135.7 2.0 copy-start
  143.3 3.8 %copy-start.1 = (f32[2,8,128,128,4]{3,2,4,1,0:T(8,128)S(1)}, f32[2,8,128,128,4]{3,2,4,1,0:T(8,128)}, u32[]{:S(2)}) copy-start(f32[2,8,128,128,4]{3,2,4,1,0:T(8,128)} %copy-done) | copy-start | bytes 12582916 | tf_op jit(solution)/shard_map/while
  170.0 4.6 %copy-start.2 = (bf16[8,128,2,128,1]{1,3,0,4,2:T(8,128)(2,1)}, bf16[8,128,2,128,1]{1,3,0,4,2:T(8,128)(2,1)S(1)}, u32[]{:S(2)}) copy-start(bf16[8,128,2,128,1]{1,3,0,4,2:T(8,128)(2,1)S(1)} %copy.184) | copy-start | bytes 1572868 | tf_op jit(solution)/shard_map/while
  173.6 2.0 copy-start
  181.2 3.8 %copy-start.1 = (f32[2,8,128,128,4]{3,2,4,1,0:T(8,128)S(1)}, f32[2,8,128,128,4]{3,2,4,1,0:T(8,128)}, u32[]{:S(2)}) copy-start(f32[2,8,128,128,4]{3,2,4,1,0:T(8,128)} %copy-done) | copy-start | bytes 12582916 | tf_op jit(solution)/shard_map/while
  218.8 12.9 %copy-start.3 = (bf16[4,128,2,4,128]{1,4,3,2,0:T(8,128)(2,1)S(1)}, bf16[4,128,2,4,128]{1,4,3,2,0:T(8,128)(2,1)}, u32[]{:S(2)}) copy-start(bf16[4,128,2,4,128]{1,4,3,2,0:T(8,128)(2,1)} %get-tuple-element.165) | copy-start | bytes 3145732
  223.2 46.8 %collective-permute-start.4 = (f32[2,512,256]{2,1,0:T(8,128)}, f32[2,512,256]{2,1,0:T(8,128)S(1)}, u32[]{:S(2)}, u32[]{:S(2)}) collective-permute-start(f32[2,512,256]{2,1,0:T(8,128)} %get-tuple-element.234), channel_id=1, source_target_pairs={{0,4},{4,8},{8,12},{12,16},{16,20},{20,24},{24,28},{28,0},{1,5},{5... | collective-permute-start | bytes 3145736 | tf_op jit(solution)/shard_map/ppermute | solution.py:16
  224.7 47.4 %collective-permute-start.5 = (f32[2,512,256]{2,1,0:T(8,128)}, f32[2,512,256]{2,1,0:T(8,128)S(1)}, u32[]{:S(2)}, u32[]{:S(2)}) collective-permute-start(f32[2,512,256]{2,1,0:T(8,128)} %get-tuple-element.235), channel_id=1, source_target_pairs={{0,28},{4,0},{8,4},{12,8},{16,12},{20,16},{24,20},{28,24},{1,29},{... | collective-permute-start | bytes 3145736 | tf_op jit(solution)/shard_map/ppermute | solution.py:16
  228.0 50.1 %collective-permute-start.6 = (f32[2,512,256]{2,1,0:T(8,128)}, f32[2,512,256]{2,1,0:T(8,128)}, u32[]{:S(2)}, u32[]{:S(2)}) collective-permute-start(f32[2,512,256]{2,1,0:T(8,128)} %get-tuple-element.237), channel_id=1, source_target_pairs={{0,8},{4,12},{8,16},{12,20},{16,24},{20,28},{24,0},{28,4},{1,9},{5... | collective-permute-start | bytes 3145736 | tf_op jit(solution)/shard_map/ppermute | solution.py:16
  228.0 67.6 %collective-permute-start.7 = (f32[2,512,256]{2,1,0:T(8,128)}, f32[2,512,256]{2,1,0:T(8,128)}, u32[]{:S(2)}, u32[]{:S(2)}) collective-permute-start(f32[2,512,256]{2,1,0:T(8,128)} %get-tuple-element.236), channel_id=1, source_target_pairs={{0,24},{4,28},{8,0},{12,4},{16,8},{20,12},{24,16},{28,20},{1,25},{... | collective-permute-start | bytes 3145736 | tf_op jit(solution)/shard_map/ppermute | solution.py:16
  233.1 65.4 %all-to-all-start = ((bf16[4,128,1024]{2,1,0:T(8,128)(2,1)}), bf16[4,128,1024]{2,1,0:T(8,128)(2,1)S(1)}, u32[]{:S(2)}, u32[]{:S(2)}) async-start(bf16[4,128,1024]{2,1,0:T(8,128)(2,1)} %copy.134), calls=%async_computation | async-start | bytes 2097152 | tf_op jit(solution)/shard_map/all_to_all | solution.py:110
  307.0 9.4 %all-to-all-start.2 = ((bf16[4,128,256]{2,1,0:T(8,128)(2,1)}), bf16[4,128,256]{2,1,0:T(8,128)(2,1)S(1)}, u32[]{:S(2)}, u32[]{:S(2)}) async-start(bf16[4,128,256]{2,1,0:T(8,128)(2,1)} %bitcast.44), calls=%async_computation.2 | async-start | bytes 524288 | tf_op jit(solution)/shard_map/all_to_all | solution.py:112
where the time goes:
time: 319 us; the launch traced here: 317 us
  local copies, waits for them, and re-layouts  103 us (32%)
  waiting for transfers between devices  84.5 us (26%)
  other arithmetic  48.6 us (15%)
  matrix products  47.8 us (15%)
  starting transfers between devices  23.5 us (7%)
  blocking collectives  8.58 us (3%)
    ppermute x8, waiting for transfers between devices, from_behind(): return lax.ppermute(x, axis, [(i, (i + by) % size) for i in range(size)])  81.5 us
    ppermute x8, starting transfers between devices, from_behind(): return lax.ppermute(x, axis, [(i, (i + by) % size) for i in range(size)])  16.6 us
    squeeze x4, local copies, waits for them, and re-layouts, one_block(): kblock = extended[0][slot_blocks]  16.1 us
    dot_general x4, matrix products, one_block(): jnp.einsum('rhgd,schd->hgrsc', orows, vblock, preferred_element_type=jnp....  15.1 us
    scatter-add x4, other arithmetic, one_block(): gradients = gradients.at[0, slot_blocks].add(dkey_part)  15.1 us
    scatter-add x4, other arithmetic, one_block(): gradients = gradients.at[1, slot_blocks].add(dvalue_part)  13.5 us
    dot_general x4, matrix products, one_block(): jnp.einsum('hgrsc,schd->rhgd', dscores, kblock, preferred_element_type=jn...  11.8 us
    mul x4, local copies, waits for them, and re-layouts, one_block(): softmax_scale * jnp.einsum('hgrsc,rhgd->schd', dscores, qrows, preferred_...  10.3 us
  transfers between devices with their start and end apart: 10, of which 8 were waited for; matrix products, arithmetic and copies ran while one was open for 5% of the time, Pallas kernels for 0%

commit v1 on v0

v1 whole, which is shorter than its diff:
```python
import functools
import math

import jax
import jax.numpy as jnp
from jax import lax
from jax.experimental import pallas as pl
from jax.experimental.pallas import tpu as pltpu
from jax.sharding import PartitionSpec as P

HEAD_SIZE = 128
BLOCK_TOKENS = 128
SLOTS = 8
REACH = 2
SHARDS = 2 * REACH + 1
F32 = jnp.float32
BF16 = jnp.bfloat16
ROWS_BY_ROWS = (((1,), (1,)), ((), ()))
COLS_BY_COLS = (((0,), (0,)), ((), ()))


def attention_kernel(
    cycle_blocks, blocks_ref, counts_ref, me_ref, queries_hbm, outgrad_hbm, *refs
):
    window_hbm = refs[:SHARDS]
    dqueries_ref = refs[SHARDS]
    partial_refs = refs[SHARDS + 1 : 2 * SHARDS + 1]
    (
        queries,
        outgrad,
        window,
        sums,
        scores_ref,
        dprobs_ref,
        probs_ref,
        block_keys,
        block_values,
        sems,
    ) = refs[2 * SHARDS + 1 :]
    tokens, query_width = queries.shape
    kv_width = window.shape[2]
    kv_heads, group = kv_width // HEAD_SIZE, query_width // kv_width
    own_blocks, rows = tokens // BLOCK_TOKENS, group * BLOCK_TOKENS
    scale = 1.0 / math.sqrt(HEAD_SIZE)
    scale_log2 = scale * math.log2(math.e)

    copies = [
        pltpu.make_async_copy(queries_hbm, queries, sems.at[0]),
        pltpu.make_async_copy(outgrad_hbm, outgrad, sems.at[1]),
    ]
    for j in range(SHARDS):
        place = window.at[:, pl.ds(j * tokens, tokens), :]
        copies.append(pltpu.make_async_copy(window_hbm[j], place, sems.at[2 + j]))
    for copy in copies:
        copy.start()
    sums[...] = jnp.zeros_like(sums)
    for copy in copies:
        copy.wait()
    first_block = (me_ref[0] - REACH) * own_blocks

    def head_block(qblock, head, live):
        row_ds = pl.ds(pl.multiple_of(qblock * BLOCK_TOKENS, BLOCK_TOKENS), BLOCK_TOKENS)
        kv_cols = slice(head * HEAD_SIZE, (head + 1) * HEAD_SIZE)
        q_cols = [
            slice((head * group + g) * HEAD_SIZE, (head * group + g + 1) * HEAD_SIZE)
            for g in range(group)
        ]
        slots = [slice(s * BLOCK_TOKENS, (s + 1) * BLOCK_TOKENS) for s in range(live)]
        places = []
        for s in range(live):
            place = lax.rem(blocks_ref[qblock, s] - first_block + cycle_blocks, cycle_blocks)
            place = pl.ds(pl.multiple_of(place * BLOCK_TOKENS, BLOCK_TOKENS), BLOCK_TOKENS)
            places.append(place)
            block_keys[slots[s]] = window[0, place, kv_cols]
            block_values[slots[s]] = window[1, place, kv_cols]
        q = jnp.concatenate([queries[row_ds, c] for c in q_cols], axis=0)
        o = jnp.concatenate([outgrad[row_ds, c] for c in q_cols], axis=0)

        def fold(x, op):
            return op(x.reshape(BLOCK_TOKENS // 8, 8, rows), axis=0)

        top = None
        for s in range(live):
            scores = lax.dot_general(
                block_keys[slots[s]], q, ROWS_BY_ROWS, preferred_element_type=F32
            )
            scores_ref[slots[s]] = scores
            part = fold(scores, jnp.max)
            top = part if s == 0 else jnp.maximum(top, part)
        row_max = jnp.max(top, axis=0, keepdims=True) * scale_log2
        total = weighted = None
        for s in range(live):
            dprobs = lax.dot_general(
                block_values[slots[s]], o, ROWS_BY_ROWS, preferred_element_type=F32
            )
            weights = jnp.exp2(scores_ref[slots[s]] * scale_log2 - row_max)
            dprobs_ref[slots[s]] = dprobs
            probs_ref[slots[s]] = weights.astype(BF16)
            part, wpart = fold(weights, jnp.sum), fold(weights * dprobs, jnp.sum)
            total = part if s == 0 else total + part
            weighted = wpart if s == 0 else weighted + wpart
        inverse = 1.0 / jnp.sum(total, axis=0, keepdims=True)
        row_delta = jnp.sum(weighted, axis=0, keepdims=True) * inverse
        inverse_col = jnp.transpose(jnp.broadcast_to(inverse, (8, rows)))[:, :1]
        q_scaled = (q.astype(F32) * inverse_col).astype(BF16)
        o_scaled = (o.astype(F32) * inverse_col).astype(BF16)
        dq = None
        for s in range(live):
            weights = probs_ref[slots[s]]
            dscores = (weights.astype(F32) * (dprobs_ref[slots[s]] - row_delta)).astype(BF16)
            sums[0, places[s], kv_cols] += jnp.dot(
                dscores, q_scaled, preferred_element_type=F32
            )
            sums[1, places[s], kv_cols] += jnp.dot(
                weights, o_scaled, preferred_element_type=F32
            )
            part = lax.dot_general(
                block_keys[slots[s]], dscores, COLS_BY_COLS, preferred_element_type=F32
            )
            dq = part if s == 0 else dq + part
        dq = jnp.transpose(dq * (inverse * scale)).astype(BF16)
        for g in range(group):
            dqueries_ref[row_ds, q_cols[g]] = dq[g * BLOCK_TOKENS : (g + 1) * BLOCK_TOKENS]

    def one_block(qblock, carry):
        for head in range(kv_heads):
            for live in range(1, SLOTS + 1):
                pl.when(counts_ref[qblock] == live)(
                    functools.partial(head_block, qblock, head, live)
                )
        return carry

    lax.fori_loop(0, own_blocks, one_block, 0)
    for j in range(SHARDS):
        span = slice(j * tokens, (j + 1) * tokens)
        partial_refs[j][0] = (sums[0, span] * scale).astype(BF16)
        partial_refs[j][1] = sums[1, span].astype(BF16)


def attention(cycle_blocks, blocks, counts, me, queries, output_gradient, window):
    tokens, query_width = queries.shape
    kv_width = window[0].shape[2]
    rows = query_width // kv_width * BLOCK_TOKENS
    vmem = pl.BlockSpec(memory_space=pltpu.VMEM)
    smem = pl.BlockSpec(memory_space=pltpu.SMEM)
    hbm = pl.BlockSpec(memory_space=pl.ANY)
    return pl.pallas_call(
        functools.partial(attention_kernel, cycle_blocks),
        out_shape=[jax.ShapeDtypeStruct(queries.shape, BF16)]
        + [jax.ShapeDtypeStruct(piece.shape, BF16) for piece in window],
        in_specs=[smem] * 3 + [hbm] * (2 + SHARDS),
        out_specs=[vmem] * (1 + SHARDS),
        scratch_shapes=[
            pltpu.VMEM(queries.shape, BF16),
            pltpu.VMEM(queries.shape, BF16),
            pltpu.VMEM((2, SHARDS * tokens, kv_width), BF16),
            pltpu.VMEM((2, SHARDS * tokens, kv_width), F32),
            pltpu.VMEM((SLOTS * BLOCK_TOKENS, rows), F32),
            pltpu.VMEM((SLOTS * BLOCK_TOKENS, rows), F32),
            pltpu.VMEM((SLOTS * BLOCK_TOKENS, rows), BF16),
            pltpu.VMEM((SLOTS * BLOCK_TOKENS, HEAD_SIZE), BF16),
            pltpu.VMEM((SLOTS * BLOCK_TOKENS, HEAD_SIZE), BF16),
            pltpu.SemaphoreType.DMA((2 + SHARDS,)),
        ],
        compiler_params=pltpu.CompilerParams(vmem_limit_bytes=40 * 2**20),
        cost_estimate=pl.CostEstimate(
            flops=5 * 10**9, bytes_accessed=10**7, transcendentals=4 * 10**6
        ),
    )(blocks, counts, me, queries, output_gradient, *window)


def from_behind(x, by):
    size = lax.axis_size("ctx")
    return lax.ppermute(x, "ctx", [(i, (i + by) % size) for i in range(size)])


def on_device(queries, keys, values, output_gradient, blocks, counts):
    tokens = queries.shape[0]
    cycle_blocks = lax.axis_size("ctx") * (tokens // BLOCK_TOKENS)
    me = lax.axis_index("ctx").reshape(1)
    stacked = jnp.stack([keys, values])
    offsets = range(-REACH, REACH + 1)
    window = [stacked if o == 0 else from_behind(stacked, -o) for o in offsets]
    dqueries, *partials = attention(
        cycle_blocks, blocks, counts, me, queries, output_gradient, window
    )
    summed = partials[REACH].astype(F32)
    for offset, piece in zip(offsets, partials):
        if offset != 0:
            summed = summed + from_behind(piece, offset).astype(F32)
    summed = summed.astype(BF16)

    def exchange(x):
        return lax.all_to_all(x, "head", split_axis=0, concat_axis=1, tiled=True)

    return exchange(dqueries), exchange(summed[0]), exchange(summed[1])


def solution(mesh):
    return jax.shard_map(
        on_device,
        mesh=mesh,
        in_specs=(
            P("ctx", "head"),
            P("ctx", "head"),
            P("ctx", "head"),
            P("ctx", "head"),
            P("ctx", None),
            P("ctx"),
        ),
        out_specs=(P(("ctx", "head"), None), P(("ctx", "head"), None), P(("ctx", "head"), None)),
        check_vma=False,
    )
```

time: 319 us -> 136 us (0.43)
  local copies, waits for them, and re-layouts: 103 us -> 3.79 us
  matrix products: 47.8 us -> 0 us
  other arithmetic: 48.6 us -> 1.5 us
  Pallas kernels: 0 us -> 17.8 us
  waiting for transfers between devices: 84.5 us -> 75.2 us
  blocking collectives: 8.58 us -> 17 us
  starting transfers between devices: 23.5 us -> 18 us
    dot_general x20 -> x0, matrix products: 47.8 us -> none  [the longest x4 15.1 us: one_block(): jnp.einsum('rhgd,schd->hgrsc', orows, vblock, preferred_element_type=jnp....]
    scatter-add x8 -> x0, other arithmetic: 28.6 us -> none  [the longest x4 15.1 us: one_block(): gradients = gradients.at[0, slot_blocks].add(dkey_part)]
    squeeze x5 -> x0, local copies, waits for them, and re-layouts: 20.5 us -> none  [the longest x4 16.1 us: one_block(): kblock = extended[0][slot_blocks]]
    ppermute x8, waiting for transfers between devices: 81.5 us -> 62.3 us  [from_behind(): return lax.ppermute(x, 'ctx', [(i, (i + by) % size) for i in range(size)])]
    pallas_call x0 -> x1, Pallas kernels: none -> 17.8 us  [attention(): pl.pallas_call(functools.partial(attention_kernel, cycle_blocks), out_sha...]
    reshape x4 -> x0, local copies, waits for them, and re-layouts: 15.9 us -> none  [the longest x1 7.94 us: on_device(): segments = gradients.reshape(2, 2 * REACH + 1, tok_rows, kv_width)]
    gather x12 -> x0, local copies, waits for them, and re-layouts: 14.7 us -> none  [the longest x8 8.34 us: one_block(): kblock = extended[0][slot_blocks]]
    while x25 -> x0, local copies, waits for them, and re-layouts: 13.2 us -> none  [the longest x1 9.26 us: on_device(): lax.fori_loop(0, own_blocks, one_block, (start_grads, start_dquery, start...]
  transfers between devices with their start and end apart: 10 -> 9, of which waited for: 8 -> 9; matrix products, arithmetic and copies ran while one was open for 5% -> 1% of each run, Pallas kernels for 0% -> 0%
where the time goes in v1:
time: 136 us; the launch traced here: 134 us
  waiting for transfers between devices  75.2 us (55%)
  starting transfers between devices  18 us (13%)
  Pallas kernels  17.8 us (13%)
  blocking collectives  17 us (12%)
  local copies, waits for them, and re-layouts  3.79 us (3%)
  other arithmetic  1.5 us (1%)
    ppermute x8, waiting for transfers between devices, from_behind(): return lax.ppermute(x, 'ctx', [(i, (i + by) % size) for i in range(size)])  62.3 us
    pallas_call x1, Pallas kernels, attention(): pl.pallas_call(functools.partial(attention_kernel, cycle_blocks), out_sha...  17.8 us
    all_to_all x2, blocking collectives, exchange(): return lax.all_to_all(x, 'head', split_axis=0, concat_axis=1, tiled=True)  17 us
    ppermute x8, starting transfers between devices, from_behind(): return lax.ppermute(x, 'ctx', [(i, (i + by) % size) for i in range(size)])  14.4 us
    all_to_all x1, waiting for transfers between devices, exchange(): return lax.all_to_all(x, 'head', split_axis=0, concat_axis=1, tiled=True)  13 us
    all_to_all x1, starting transfers between devices, exchange(): return lax.all_to_all(x, 'head', split_axis=0, concat_axis=1, tiled=True)  3.52 us
  transfers between devices with their start and end apart: 9, of which 9 were waited for; matrix products, arithmetic and copies ran while one was open for 1% of the time, Pallas kernels for 0%

profile of v1, /device:TPU:0, one launch (start us, length us, event | category | flops | bytes accessed | tf_op | source)
XLA Modules:
  0.0 134.0 jit_solution(12175135861788578672)
XLA Ops:
  0.6 0.0 copy-start
  0.6 1.2 pad_maximum_fusion.refs_2_
  1.8 5.1 %collective-permute-start.3 = (bf16[2,512,256]{2,1,0:T(8,128)(2,1)S(1)}, bf16[2,512,256]{2,1,0:T(8,128)(2,1)S(1)}, u32[]{:S(2)}, u32[]{:S(2)}) collective-permute-start(bf16[2,512,256]{2,1,0:T(8,128)(2,1)S(1)} %pad_maximum_fusion.refs_2_), channel_id=1, source_target_pairs={{0,24},{4,28},{8,0},{12,4},{16,8},{20,12},{24,16},{28,20},{1,25},{... | collective-permute-start | bytes 1572872 | tf_op jit(solution)/shard_map/ppermute | solution.py:174
  6.9 1.4 %collective-permute-start.2 = (bf16[2,512,256]{2,1,0:T(8,128)(2,1)S(1)}, bf16[2,512,256]{2,1,0:T(8,128)(2,1)S(1)}, u32[]{:S(2)}, u32[]{:S(2)}) collective-permute-start(bf16[2,512,256]{2,1,0:T(8,128)(2,1)S(1)} %pad_maximum_fusion.refs_2_), channel_id=1, source_target_pairs={{0,28},{4,0},{8,4},{12,8},{16,12},{20,16},{24,20},{28,24},{1,29},{... | collective-permute-start | bytes 1572872 | tf_op jit(solution)/shard_map/ppermute | solution.py:174
  8.3 0.6 collective-permute-start.1
  8.9 1.0 collective-permute-start
  9.9 0.0 copy-start.2
  9.9 0.0 copy-start.3
  9.9 9.4 %collective-permute-done.3.refs_4_ = bf16[2,512,256]{2,1,0:T(8,128)(2,1)S(1)} collective-permute-done((bf16[2,512,256]{2,1,0:T(8,128)(2,1)S(1)}, bf16[2,512,256]{2,1,0:T(8,128)(2,1)S(1)}, u32[]{:S(2)}, u32[]{:S(2)}) %collective-permute-start.3) | collective-permute-done | bytes 524320 | tf_op jit(solution)/shard_map/ppermute | solution.py:174
  19.3 11.4 %collective-permute-done.2.refs_3_ = bf16[2,512,256]{2,1,0:T(8,128)(2,1)S(1)} collective-permute-done((bf16[2,512,256]{2,1,0:T(8,128)(2,1)S(1)}, bf16[2,512,256]{2,1,0:T(8,128)(2,1)S(1)}, u32[]{:S(2)}, u32[]{:S(2)}) %collective-permute-start.2) | collective-permute-done | bytes 524320 | tf_op jit(solution)/shard_map/ppermute | solution.py:174
  30.7 1.6 %collective-permute-done.1.refs_1_ = bf16[2,512,256]{2,1,0:T(8,128)(2,1)S(1)} collective-permute-done((bf16[2,512,256]{2,1,0:T(8,128)(2,1)S(1)}, bf16[2,512,256]{2,1,0:T(8,128)(2,1)S(1)}, u32[]{:S(2)}, u32[]{:S(2)}) %collective-permute-start.1) | collective-permute-done | bytes 524320 | tf_op jit(solution)/shard_map/ppermute | solution.py:174
  32.3 9.3 %collective-permute-done.refs_0_ = bf16[2,512,256]{2,1,0:T(8,128)(2,1)} collective-permute-done((bf16[2,512,256]{2,1,0:T(8,128)(2,1)S(1)}, bf16[2,512,256]{2,1,0:T(8,128)(2,1)}, u32[]{:S(2)}, u32[]{:S(2)}) %collective-permute-start) | collective-permute-done | bytes 524320 | tf_op jit(solution)/shard_map/ppermute | solution.py:174
  41.6 0.0 copy-done
  41.6 0.0 copy-done.2
  41.6 0.0 copy-done.3
  41.6 0.0 copy-start.1
  41.6 1.2 copy-done.1
  42.9 17.8 %shard_map.85 = (bf16[512,1024]{1,0:T(8,128)(2,1)}, bf16[2,512,256]{2,1,0:T(8,128)(2,1)S(1)}, bf16[2,512,256]{2,1,0:T(8,128)(2,1)S(1)}, bf16[2,512,256]{2,1,0:T(...) custom-call(s32[4,8]{1,0:T(4,128)S(1)} %copy-done.2, s32[4]{0:T(128)S(1)} %copy-done.3, ...), custom_call_target="tpu_custom_call" | custom-call | flops 5000000000 | bytes 10000000 | tf_op jit(solution)/shard_map/pallas_call | solution.py:147
  60.7 1.5 %collective-permute-start.4 = (bf16[2,512,256]{2,1,0:T(8,128)(2,1)S(1)}, bf16[2,512,256]{2,1,0:T(8,128)(2,1)S(1)}, u32[]{:S(2)}, u32[]{:S(2)}) collective-permute-start(bf16[2,512,256]{2,1,0:T(8,128)(2,1)S(1)} %get-tuple-element.11), channel_id=1, source_target_pairs={{0,24},{4,28},{8,0},{12,4},{16,8},{20,12},{24,16},{28,20},{1,25},{... | collective-permute-start | bytes 1572872 | tf_op jit(solution)/shard_map/ppermute | solution.py:174
  62.2 4.9 %collective-permute-start.5 = (bf16[2,512,256]{2,1,0:T(8,128)(2,1)S(1)}, bf16[2,512,256]{2,1,0:T(8,128)(2,1)S(1)}, u32[]{:S(2)}, u32[]{:S(2)}) collective-permute-start(bf16[2,512,256]{2,1,0:T(8,128)(2,1)S(1)} %get-tuple-element.12), channel_id=1, source_target_pairs={{0,28},{4,0},{8,4},{12,8},{16,12},{20,16},{24,20},{28,24},{1,29},{... | collective-permute-start | bytes 1572872 | tf_op jit(solution)/shard_map/ppermute | solution.py:174
  67.1 0.0 collective-permute-start.6
  67.1 0.0 collective-permute-start.7
  67.1 8.6 %collective-permute-done.4 = bf16[2,512,256]{2,1,0:T(8,128)(2,1)S(1)} collective-permute-done((bf16[2,512,256]{2,1,0:T(8,128)(2,1)S(1)}, bf16[2,512,256]{2,1,0:T(8,128)(2,1)S(1)}, u32[]{:S(2)}, u32[]{:S(2)}) %collective-permute-start.4) | collective-permute-done | bytes 524320 | tf_op jit(solution)/shard_map/ppermute | solution.py:174
  75.6 10.2 %collective-permute-done.5 = bf16[2,512,256]{2,1,0:T(8,128)(2,1)S(1)} collective-permute-done((bf16[2,512,256]{2,1,0:T(8,128)(2,1)S(1)}, bf16[2,512,256]{2,1,0:T(8,128)(2,1)S(1)}, u32[]{:S(2)}, u32[]{:S(2)}) %collective-permute-start.5) | collective-permute-done | bytes 524320 | tf_op jit(solution)/shard_map/ppermute | solution.py:174
  85.9 5.3 %collective-permute-done.6 = bf16[2,512,256]{2,1,0:T(8,128)(2,1)S(1)} collective-permute-done((bf16[2,512,256]{2,1,0:T(8,128)(2,1)S(1)}, bf16[2,512,256]{2,1,0:T(8,128)(2,1)S(1)}, u32[]{:S(2)}, u32[]{:S(2)}) %collective-permute-start.6) | collective-permute-done | bytes 524320 | tf_op jit(solution)/shard_map/ppermute | solution.py:174
  91.1 6.5 %collective-permute-done.7 = bf16[2,512,256]{2,1,0:T(8,128)(2,1)S(1)} collective-permute-done((bf16[2,512,256]{2,1,0:T(8,128)(2,1)S(1)}, bf16[2,512,256]{2,1,0:T(8,128)(2,1)S(1)}, u32[]{:S(2)}, u32[]{:S(2)}) %collective-permute-start.7) | collective-permute-done | bytes 524320 | tf_op jit(solution)/shard_map/ppermute | solution.py:174
  97.6 0.3 add_convert_fusion
  98.0 8.6 %all_to_all.57 = bf16[4,128,256]{2,1,0:T(8,128)(2,1)S(1)} all-to-all(bf16[4,128,256]{2,1,0:T(8,128)(2,1)S(1)} %bitcast.20), channel_id=1, replica_groups=mesh['ctx'=8,'head'=4] {'head'}, dimensions={0} | all-to-all | bytes 524288 | tf_op jit(solution)/shard_map/all_to_all | solution.py:194
  106.6 8.4 %all_to_all.58 = bf16[4,128,256]{2,1,0:T(8,128)(2,1)S(1)} all-to-all(bf16[4,128,256]{2,1,0:T(8,128)(2,1)S(1)} %bitcast.19), channel_id=1, replica_groups=mesh['ctx'=8,'head'=4] {'head'}, dimensions={0} | all-to-all | bytes 524288 | tf_op jit(solution)/shard_map/all_to_all | solution.py:194
  115.0 3.5 %all-to-all-start = ((bf16[4,128,1024]{2,1,0:T(8,128)(2,1)}), bf16[4,128,1024]{2,1,0:T(8,128)(2,1)S(1)}, u32[]{:S(2)}, u32[]{:S(2)}) async-start(bf16[4,128,1024]{2,1,0:T(8,128)(2,1)} %bitcast.3), calls=%async_computation | async-start | bytes 2097152 | tf_op jit(solution)/shard_map/all_to_all | solution.py:194
  118.5 0.7 copy.13
  119.3 0.7 copy.14
  120.0 13.0 %all-to-all-done = bf16[4,128,1024]{2,1,0:T(8,128)(2,1)S(1)} async-done(((bf16[4,128,1024]{2,1,0:T(8,128)(2,1)}), bf16[4,128,1024]{2,1,0:T(8,128)(2,1)S(1)}, u32[]{:S(2)}, u32[]{:S(2)}) %all-to-all-start) | async-done | bytes 1048608 | tf_op jit(solution)/shard_map/all_to_all | solution.py:194
  133.0 1.1 copy.12
  (1 shorter events, 0.0 us)
Async XLA Ops:
  0.6 41.0 %copy-start = (bf16[512,1024]{1,0:T(8,128)(2,1)S(1)}, bf16[512,1024]{1,0:T(8,128)(2,1)}, u32[]{:S(2)}) copy-start(bf16[512,1024]{1,0:T(8,128)(2,1)} %queries_hbm.1) | copy-start | bytes 3145732
  1.8 17.5 %collective-permute-start.3 = (bf16[2,512,256]{2,1,0:T(8,128)(2,1)S(1)}, bf16[2,512,256]{2,1,0:T(8,128)(2,1)S(1)}, u32[]{:S(2)}, u32[]{:S(2)}) collective-permute-start(bf16[2,512,256]{2,1,0:T(8,128)(2,1)S(1)} %pad_maximum_fusion.refs_2_), channel_id=1, source_target_pairs={{0,24},{4,28},{8,0},{12,4},{16,8},{20,12},{24,16},{28,20},{1,25},{... | collective-permute-start | bytes 1572872 | tf_op jit(solution)/shard_map/ppermute | solution.py:174
  6.9 23.8 %collective-permute-start.2 = (bf16[2,512,256]{2,1,0:T(8,128)(2,1)S(1)}, bf16[2,512,256]{2,1,0:T(8,128)(2,1)S(1)}, u32[]{:S(2)}, u32[]{:S(2)}) collective-permute-start(bf16[2,512,256]{2,1,0:T(8,128)(2,1)S(1)} %pad_maximum_fusion.refs_2_), channel_id=1, source_target_pairs={{0,28},{4,0},{8,4},{12,8},{16,12},{20,16},{24,20},{28,24},{1,29},{... | collective-permute-start | bytes 1572872 | tf_op jit(solution)/shard_map/ppermute | solution.py:174
  8.3 24.0 %collective-permute-start.1 = (bf16[2,512,256]{2,1,0:T(8,128)(2,1)S(1)}, bf16[2,512,256]{2,1,0:T(8,128)(2,1)S(1)}, u32[]{:S(2)}, u32[]{:S(2)}) collective-permute-start(bf16[2,512,256]{2,1,0:T(8,128)(2,1)S(1)} %pad_maximum_fusion.refs_2_), channel_id=1, source_target_pairs={{0,4},{4,8},{8,12},{12,16},{16,20},{20,24},{24,28},{28,0},{1,5},{5... | collective-permute-start | bytes 1572872 | tf_op jit(solution)/shard_map/ppermute | solution.py:174
  8.9 32.7 %collective-permute-start = (bf16[2,512,256]{2,1,0:T(8,128)(2,1)S(1)}, bf16[2,512,256]{2,1,0:T(8,128)(2,1)}, u32[]{:S(2)}, u32[]{:S(2)}) collective-permute-start(bf16[2,512,256]{2,1,0:T(8,128)(2,1)S(1)} %pad_maximum_fusion.refs_2_), channel_id=1, source_target_pairs={{0,8},{4,12},{8,16},{12,20},{16,24},{20,28},{24,0},{28,4},{1,9},{5... | collective-permute-start | bytes 1572872 | tf_op jit(solution)/shard_map/ppermute | solution.py:174
  9.9 31.7 %copy-start.2 = (s32[4,8]{1,0:T(4,128)S(1)}, s32[4,8]{1,0:T(4,128)}, u32[]{:S(2)}) copy-start(s32[4,8]{1,0:T(4,128)} %blocks_ref.1) | copy-start | bytes 388
  9.9 31.7 %copy-start.3 = (s32[4]{0:T(128)S(1)}, s32[4]{0:T(128)}, u32[]{:S(2)}) copy-start(s32[4]{0:T(128)} %counts_ref.1) | copy-start | bytes 52
  41.6 1.2 copy-start.1
  60.7 14.9 %collective-permute-start.4 = (bf16[2,512,256]{2,1,0:T(8,128)(2,1)S(1)}, bf16[2,512,256]{2,1,0:T(8,128)(2,1)S(1)}, u32[]{:S(2)}, u32[]{:S(2)}) collective-permute-start(bf16[2,512,256]{2,1,0:T(8,128)(2,1)S(1)} %get-tuple-element.11), channel_id=1, source_target_pairs={{0,24},{4,28},{8,0},{12,4},{16,8},{20,12},{24,16},{28,20},{1,25},{... | collective-permute-start | bytes 1572872 | tf_op jit(solution)/shard_map/ppermute | solution.py:174
  62.2 23.7 %collective-permute-start.5 = (bf16[2,512,256]{2,1,0:T(8,128)(2,1)S(1)}, bf16[2,512,256]{2,1,0:T(8,128)(2,1)S(1)}, u32[]{:S(2)}, u32[]{:S(2)}) collective-permute-start(bf16[2,512,256]{2,1,0:T(8,128)(2,1)S(1)} %get-tuple-element.12), channel_id=1, source_target_pairs={{0,28},{4,0},{8,4},{12,8},{16,12},{20,16},{24,20},{28,24},{1,29},{... | collective-permute-start | bytes 1572872 | tf_op jit(solution)/shard_map/ppermute | solution.py:174
  67.1 24.1 %collective-permute-start.6 = (bf16[2,512,256]{2,1,0:T(8,128)(2,1)S(1)}, bf16[2,512,256]{2,1,0:T(8,128)(2,1)S(1)}, u32[]{:S(2)}, u32[]{:S(2)}) collective-permute-start(bf16[2,512,256]{2,1,0:T(8,128)(2,1)S(1)} %get-tuple-element.13), channel_id=1, source_target_pairs={{0,4},{4,8},{8,12},{12,16},{16,20},{20,24},{24,28},{28,0},{1,5},{5... | collective-permute-start | bytes 1572872 | tf_op jit(solution)/shard_map/ppermute | solution.py:174
  67.1 30.6 %collective-permute-start.7 = (bf16[2,512,256]{2,1,0:T(8,128)(2,1)S(1)}, bf16[2,512,256]{2,1,0:T(8,128)(2,1)S(1)}, u32[]{:S(2)}, u32[]{:S(2)}) collective-permute-start(bf16[2,512,256]{2,1,0:T(8,128)(2,1)S(1)} %get-tuple-element.14), channel_id=1, source_target_pairs={{0,8},{4,12},{8,16},{12,20},{16,24},{20,28},{24,0},{28,4},{1,9},{5... | collective-permute-start | bytes 1572872 | tf_op jit(solution)/shard_map/ppermute | solution.py:174
  115.0 18.0 %all-to-all-start = ((bf16[4,128,1024]{2,1,0:T(8,128)(2,1)}), bf16[4,128,1024]{2,1,0:T(8,128)(2,1)S(1)}, u32[]{:S(2)}, u32[]{:S(2)}) async-start(bf16[4,128,1024]{2,1,0:T(8,128)(2,1)} %bitcast.3), calls=%async_computation | async-start | bytes 2097152 | tf_op jit(solution)/shard_map/all_to_all | solution.py:194

commit v2 on v1

v2 whole, which is shorter than its diff:
```python
import functools
import math

import jax
import jax.numpy as jnp
from jax import lax
from jax.experimental import pallas as pl
from jax.experimental.pallas import tpu as pltpu
from jax.sharding import PartitionSpec as P

HEAD_SIZE = 128
BLOCK_TOKENS = 128
SLOTS = 8
REACH = 2
SHARDS = 2 * REACH + 1
F32 = jnp.float32
BF16 = jnp.bfloat16
ROWS_BY_ROWS = (((1,), (1,)), ((), ()))
COLS_BY_COLS = (((0,), (0,)), ((), ()))


def attention_kernel(
    head, cycle_blocks, places_out, blocks_ref, counts_ref, me_ref, queries_hbm, outgrad_hbm, *refs
):
    window_hbm = refs[:SHARDS]
    dqueries_refs = refs[SHARDS : SHARDS + places_out]
    partial_refs = refs[SHARDS + places_out : 2 * SHARDS + places_out]
    (
        dqueries_ref,
        queries,
        outgrad,
        window,
        sums,
        scores_ref,
        dprobs_ref,
        block_keys,
        block_values,
        sems,
    ) = refs[2 * SHARDS + places_out :]
    tokens, query_width = queries.shape
    group = query_width // HEAD_SIZE
    own_blocks, rows = tokens // BLOCK_TOKENS, group * BLOCK_TOKENS
    scale = 1.0 / math.sqrt(HEAD_SIZE)
    scale_log2 = scale * math.log2(math.e)

    columns = pl.ds(head * query_width, query_width)
    copies = [
        pltpu.make_async_copy(queries_hbm.at[:, columns], queries, sems.at[0]),
        pltpu.make_async_copy(outgrad_hbm.at[:, columns], outgrad, sems.at[1]),
    ]
    for j in range(SHARDS):
        place = window.at[:, pl.ds(j * tokens, tokens), :]
        copies.append(pltpu.make_async_copy(window_hbm[j], place, sems.at[2 + j]))
    for copy in copies:
        copy.start()
    sums[...] = jnp.zeros_like(sums)
    for copy in copies:
        copy.wait()
    first_block = (me_ref[0] - REACH) * own_blocks

    def query_block(qblock, live):
        row_ds = pl.ds(pl.multiple_of(qblock * BLOCK_TOKENS, BLOCK_TOKENS), BLOCK_TOKENS)
        q_cols = [slice(g * HEAD_SIZE, (g + 1) * HEAD_SIZE) for g in range(group)]
        slots = [slice(s * BLOCK_TOKENS, (s + 1) * BLOCK_TOKENS) for s in range(live)]
        places = []
        for s in range(live):
            place = lax.rem(blocks_ref[qblock, s] - first_block + cycle_blocks, cycle_blocks)
            place = pl.ds(pl.multiple_of(place * BLOCK_TOKENS, BLOCK_TOKENS), BLOCK_TOKENS)
            places.append(place)
            block_keys[slots[s]] = window[0, place]
            block_values[slots[s]] = window[1, place]
        q = jnp.concatenate([queries[row_ds, c] for c in q_cols], axis=0)
        o = jnp.concatenate([outgrad[row_ds, c] for c in q_cols], axis=0)

        def fold(x, op):
            return op(x.reshape(BLOCK_TOKENS // 8, 8, rows), axis=0)

        top = None
        for s in range(live):
            scores = lax.dot_general(
                block_keys[slots[s]], q, ROWS_BY_ROWS, preferred_element_type=F32
            )
            scores_ref[slots[s]] = scores
            part = fold(scores, jnp.max)
            top = part if s == 0 else jnp.maximum(top, part)
        row_max = jnp.max(top, axis=0, keepdims=True) * scale_log2
        total = weighted = None
        for s in range(live):
            dprobs = lax.dot_general(
                block_values[slots[s]], o, ROWS_BY_ROWS, preferred_element_type=F32
            )
            weights = jnp.exp2(scores_ref[slots[s]] * scale_log2 - row_max)
            dprobs_ref[slots[s]] = dprobs
            scores_ref[slots[s]] = weights
            part, wpart = fold(weights, jnp.sum), fold(weights * dprobs, jnp.sum)
            total = part if s == 0 else total + part
            weighted = wpart if s == 0 else weighted + wpart
        inverse = 1.0 / jnp.sum(total, axis=0, keepdims=True)
        row_delta = jnp.sum(weighted, axis=0, keepdims=True) * inverse
        dq = None
        for s in range(live):
            probs = scores_ref[slots[s]] * inverse
            dscores = (probs * (dprobs_ref[slots[s]] - row_delta)).astype(BF16)
            sums[0, places[s]] += jnp.dot(dscores, q, preferred_element_type=F32)
            sums[1, places[s]] += jnp.dot(
                probs.astype(BF16), o, preferred_element_type=F32
            )
            part = lax.dot_general(
                block_keys[slots[s]], dscores, COLS_BY_COLS, preferred_element_type=F32
            )
            dq = part if s == 0 else dq + part
        dq = jnp.transpose(dq * scale).astype(BF16)
        for g in range(group):
            dqueries_ref[row_ds, q_cols[g]] = dq[g * BLOCK_TOKENS : (g + 1) * BLOCK_TOKENS]

    def one_block(qblock, carry):
        for live in range(1, SLOTS + 1):
            pl.when(counts_ref[qblock] == live)(functools.partial(query_block, qblock, live))
        return carry

    lax.fori_loop(0, own_blocks, one_block, 0)
    share = tokens // places_out
    for k in range(places_out):
        first = pl.multiple_of((me_ref[1] ^ k) * share, share)
        dqueries_refs[k][...] = dqueries_ref[pl.ds(first, share)]
    for j in range(SHARDS):
        span = slice(j * tokens, (j + 1) * tokens)
        partial_refs[j][0] = (sums[0, span] * scale).astype(BF16)
        partial_refs[j][1] = sums[1, span].astype(BF16)


def attention(head, heads, cycle_blocks, places_out, blocks, counts, me, queries, output_gradient, window):
    tokens, query_width = queries.shape
    query_width //= heads
    kv_width = window[0].shape[2]
    rows = query_width // kv_width * BLOCK_TOKENS
    vmem = pl.BlockSpec(memory_space=pltpu.VMEM)
    smem = pl.BlockSpec(memory_space=pltpu.SMEM)
    hbm = pl.BlockSpec(memory_space=pl.ANY)
    return pl.pallas_call(
        functools.partial(attention_kernel, head, cycle_blocks, places_out),
        out_shape=[jax.ShapeDtypeStruct((tokens // places_out, query_width), BF16)] * places_out
        + [jax.ShapeDtypeStruct(piece.shape, BF16) for piece in window],
        in_specs=[smem] * 3 + [hbm] * (2 + SHARDS),
        out_specs=[vmem] * (places_out + SHARDS),
        scratch_shapes=[
            pltpu.VMEM((tokens, query_width), BF16),
            pltpu.VMEM((tokens, query_width), BF16),
            pltpu.VMEM((tokens, query_width), BF16),
            pltpu.VMEM((2, SHARDS * tokens, kv_width), BF16),
            pltpu.VMEM((2, SHARDS * tokens, kv_width), F32),
            pltpu.VMEM((SLOTS * BLOCK_TOKENS, rows), F32),
            pltpu.VMEM((SLOTS * BLOCK_TOKENS, rows), F32),
            pltpu.VMEM((SLOTS * BLOCK_TOKENS, HEAD_SIZE), BF16),
            pltpu.VMEM((SLOTS * BLOCK_TOKENS, HEAD_SIZE), BF16),
            pltpu.SemaphoreType.DMA((2 + SHARDS,)),
        ],
        compiler_params=pltpu.CompilerParams(vmem_limit_bytes=20 * 2**20),
        cost_estimate=pl.CostEstimate(
            flops=2 * 10**9, bytes_accessed=2 * 10**7, transcendentals=2 * 10**6
        ),
    )(blocks, counts, me, queries, output_gradient, *window)


def sum_kernel(me_ref, *refs):
    parts, outs = refs[:SHARDS], refs[SHARDS:]
    share = outs[0].shape[1]
    for k, out in enumerate(outs):
        rows = pl.ds(pl.multiple_of((me_ref[1] ^ k) * share, share), share)
        total = parts[0][:, rows].astype(F32)
        for part in parts[1:]:
            total = total + part[:, rows].astype(F32)
        out[...] = total.astype(BF16)


def sum_parts(me, parts, places_out):
    _, tokens, width = parts[0].shape
    vmem = pl.BlockSpec(memory_space=pltpu.VMEM)
    smem = pl.BlockSpec(memory_space=pltpu.SMEM)
    piece = jax.ShapeDtypeStruct((2, tokens // places_out, width), BF16)
    return pl.pallas_call(
        sum_kernel,
        out_shape=[piece] * places_out,
        in_specs=[smem] + [vmem] * SHARDS,
        out_specs=[vmem] * places_out,
        compiler_params=pltpu.CompilerParams(vmem_limit_bytes=8 * 2**20),
    )(me, *parts)


def assemble_kernel(heads, places_out, me_ref, *refs):
    n = heads * places_out
    dq_pieces, dkv_pieces = refs[:n], refs[n : 2 * n]
    dq_out, dk_out, dv_out, sems = refs[2 * n :]
    copies = []
    for head in range(heads):
        for k in range(places_out):
            index = head * places_out + k
            place = (me_ref[1] ^ k) * heads + head
            for which, (out, source) in enumerate(
                (
                    (dq_out, dq_pieces[index]),
                    (dk_out, dkv_pieces[index].at[0]),
                    (dv_out, dkv_pieces[index].at[1]),
                )
            ):
                width = source.shape[1]
                columns = pl.ds(pl.multiple_of(place * width, width), width)
                copies.append(
                    pltpu.make_async_copy(source, out.at[:, columns], sems.at[which, index])
                )
    for copy in copies:
        copy.start()
    for copy in copies:
        copy.wait()


def assemble(me, dq_pieces, dkv_pieces, heads, places_out):
    share, query_width = dq_pieces[0].shape
    kv_width = dkv_pieces[0].shape[2]
    n = heads * places_out
    vmem = pl.BlockSpec(memory_space=pltpu.VMEM)
    hbm = pl.BlockSpec(memory_space=pl.ANY)
    smem = pl.BlockSpec(memory_space=pltpu.SMEM)
    return pl.pallas_call(
        functools.partial(assemble_kernel, heads, places_out),
        out_shape=[
            jax.ShapeDtypeStruct((share, n * query_width), BF16),
            jax.ShapeDtypeStruct((share, n * kv_width), BF16),
            jax.ShapeDtypeStruct((share, n * kv_width), BF16),
        ],
        in_specs=[smem] + [vmem] * (2 * n),
        out_specs=[hbm] * 3,
        scratch_shapes=[pltpu.SemaphoreType.DMA((3, n))],
        compiler_params=pltpu.CompilerParams(vmem_limit_bytes=8 * 2**20),
    )(me, *dq_pieces, *dkv_pieces)


def from_behind(x, by):
    size = lax.axis_size("ctx")
    return lax.ppermute(x, "ctx", [(i, (i + by) % size) for i in range(size)])


def exchange(pieces):
    return [
        piece if k == 0 else lax.ppermute(piece, "head", [(i, i ^ k) for i in range(len(pieces))])
        for k, piece in enumerate(pieces)
    ]


def on_device(queries, keys, values, output_gradient, blocks, counts):
    tokens = queries.shape[0]
    cycle_blocks = lax.axis_size("ctx") * (tokens // BLOCK_TOKENS)
    places_out = lax.axis_size("head")
    me = jnp.stack([lax.axis_index("ctx"), lax.axis_index("head")])
    heads = keys.shape[1] // HEAD_SIZE
    offsets = range(-REACH, REACH + 1)

    windows = []
    for head in range(heads):
        columns = slice(head * HEAD_SIZE, (head + 1) * HEAD_SIZE)
        own = jnp.stack([keys[:, columns], values[:, columns]])
        windows.append([own if o == 0 else from_behind(own, -o) for o in offsets])
    dq_pieces, dkv_pieces = [], []
    for head, window in enumerate(windows):
        outs = attention(
            head,
            heads,
            cycle_blocks,
            places_out,
            blocks,
            counts,
            me,
            queries,
            output_gradient,
            window,
        )
        dqueries, partials = outs[:places_out], outs[places_out:]
        parts = [p if o == 0 else from_behind(p, o) for o, p in zip(offsets, partials)]
        dq_pieces += exchange(dqueries)
        dkv_pieces += exchange(sum_parts(me, parts, places_out))
    return tuple(assemble(me, dq_pieces, dkv_pieces, heads, places_out))


def solution(mesh):
    return jax.shard_map(
        on_device,
        mesh=mesh,
        in_specs=(
            P("ctx", "head"),
            P("ctx", "head"),
            P("ctx", "head"),
            P("ctx", "head"),
            P("ctx", None),
            P("ctx"),
        ),
        out_specs=(P(("ctx", "head"), None), P(("ctx", "head"), None), P(("ctx", "head"), None)),
        check_vma=False,
    )
```

time: 136 us -> 89.5 us (0.66); the launches traced: 134 us -> 89.3 us
  waiting for transfers between devices: 75.2 us -> 33.5 us
  blocking collectives: 17 us -> 0 us
  starting transfers between devices: 18 us -> 32.1 us
  Pallas kernels: 17.8 us -> 20.8 us
  local copies, waits for them, and re-layouts: 3.79 us -> 1.88 us
  other arithmetic: 1.5 us -> 0.13 us
    ppermute x8 -> x16, waiting for transfers between devices: 62.3 us -> 28.9 us  [from_behind(): return lax.ppermute(x, 'ctx', [(i, (i + by) % size) for i in range(size)])]
    all_to_all x2 -> x0, blocking collectives: 17 us -> none  [exchange(): return lax.all_to_all(x, 'head', split_axis=0, concat_axis=1, tiled=True)]
    all_to_all x1 -> x0, waiting for transfers between devices: 13 us -> none  [exchange(): return lax.all_to_all(x, 'head', split_axis=0, concat_axis=1, tiled=True)]
    ppermute x8 -> x16, starting transfers between devices: 14.4 us -> 26.1 us  [from_behind(): return lax.ppermute(x, 'ctx', [(i, (i + by) % size) for i in range(size)])]
    ppermute x0 -> x12, starting transfers between devices: none -> 5.92 us  [exchange(): lax.ppermute(piece, 'head', [(i, i ^ k) for i in range(len(pieces))])]
    ppermute x0 -> x12, waiting for transfers between devices: none -> 4.61 us  [exchange(): lax.ppermute(piece, 'head', [(i, i ^ k) for i in range(len(pieces))])]
    all_to_all x1 -> x0, starting transfers between devices: 3.52 us -> none  [exchange(): return lax.all_to_all(x, 'head', split_axis=0, concat_axis=1, tiled=True)]
    pallas_call x1 -> x5, Pallas kernels: 17.8 us -> 20.8 us  [the longest x2 17.5 us: attention(): pl.pallas_call(functools.partial(attention_kernel, head, cycle_blocks, pl...]
  transfers between devices with their start and end apart: 9 -> 28, of which waited for: 9 -> 13; matrix products, arithmetic and copies ran while one was open for 1% -> 0% of each run, Pallas kernels for 0% -> 21%
where the time goes in v2:
time: 89.5 us; the launch traced here: 89.3 us
  waiting for transfers between devices  33.5 us (37%)
  starting transfers between devices  32.1 us (36%)
  Pallas kernels  20.8 us (23%)
  local copies, waits for them, and re-layouts  1.88 us (2%)
  between operations  0.95 us (1%)
    ppermute x16, waiting for transfers between devices, from_behind(): return lax.ppermute(x, 'ctx', [(i, (i + by) % size) for i in range(size)])  28.9 us
    ppermute x16, starting transfers between devices, from_behind(): return lax.ppermute(x, 'ctx', [(i, (i + by) % size) for i in range(size)])  26.1 us
    pallas_call x2, Pallas kernels, attention(): pl.pallas_call(functools.partial(attention_kernel, head, cycle_blocks, pl...  17.5 us
    ppermute x12, starting transfers between devices, exchange(): lax.ppermute(piece, 'head', [(i, i ^ k) for i in range(len(pieces))])  5.92 us
    ppermute x12, waiting for transfers between devices, exchange(): lax.ppermute(piece, 'head', [(i, i ^ k) for i in range(len(pieces))])  4.61 us
    pallas_call x1, Pallas kernels, assemble(): pl.pallas_call(functools.partial(assemble_kernel, heads, places_out), out...  1.87 us
  transfers between devices with their start and end apart: 28, of which 13 were waited for; matrix products, arithmetic and copies ran while one was open for 0% of the time, Pallas kernels for 21%

profile of v2, /device:TPU:0, one launch (start us, length us, event | category | flops | bytes accessed | tf_op | source)
XLA Modules:
  0.0 89.3 jit_solution(5799643464531150120)
XLA Ops:
  0.7 1.3 %slice_bitcast_fusion = (bf16[1,512,128]{2,1,0:T(8,128)(2,1)S(1)}, bf16[1,512,128]{2,1,0:T(8,128)(2,1)S(1)}, bf16[1,512,128]{2,1,0:T(8,128)(2,1)S(1)}, bf16[1,512,128]{2,1,0:T(8,128)(2,1)S(1)}) fusion(bf16[512,256]{1,0:T(8,128)(2,1)} %param.8, bf16[512,256]{1,0:T(8,128)(2,1)} %param.7), kind=kLoop, calls=%fused_computation.2 | loop fusion | bytes 1048576 | tf_op jit(solution)/shard_map/stack | solution.py:261
  2.0 5.1 %collective-permute-start.10 = (bf16[2,512,128]{2,1,0:T(8,128)(2,1)S(1)}, bf16[2,512,128]{2,1,0:T(8,128)(2,1)S(1)}, u32[]{:S(2)}, u32[]{:S(2)}) collective-permute-start(bf16[2,512,128]{2,1,0:T(8,128)(2,1)S(1)} %pad_maximum_fusion.1.refs_2_), channel_id=1, source_target_pairs={{0,24},{4,28},{8,0},{12,4},{16,8},{20,12},{24,16},{28,20},{1,25},{... | collective-permute-start | bytes 786440 | tf_op jit(solution)/shard_map/ppermute | solution.py:240
  7.1 0.0 collective-permute-start.7
  7.1 1.5 %collective-permute-start.8 = (bf16[2,512,128]{2,1,0:T(8,128)(2,1)S(1)}, bf16[2,512,128]{2,1,0:T(8,128)(2,1)}, u32[]{:S(2)}, u32[]{:S(2)}) collective-permute-start(bf16[2,512,128]{2,1,0:T(8,128)(2,1)S(1)} %pad_maximum_fusion.1.refs_2_), channel_id=1, source_target_pairs={{0,4},{4,8},{8,12},{12,16},{16,20},{20,24},{24,28},{28,0},{1,5},{5... | collective-permute-start | bytes 786440 | tf_op jit(solution)/shard_map/ppermute | solution.py:240
  8.6 3.3 %collective-permute-start.9 = (bf16[2,512,128]{2,1,0:T(8,128)(2,1)S(1)}, bf16[2,512,128]{2,1,0:T(8,128)(2,1)}, u32[]{:S(2)}, u32[]{:S(2)}) collective-permute-start(bf16[2,512,128]{2,1,0:T(8,128)(2,1)S(1)} %pad_maximum_fusion.1.refs_2_), channel_id=1, source_target_pairs={{0,28},{4,0},{8,4},{12,8},{16,12},{20,16},{24,20},{28,24},{1,29},{... | collective-permute-start | bytes 786440 | tf_op jit(solution)/shard_map/ppermute | solution.py:240
  11.9 0.1 collective-permute-start
  12.0 1.8 %collective-permute-done.10.refs_4_ = bf16[2,512,128]{2,1,0:T(8,128)(2,1)S(1)} collective-permute-done((bf16[2,512,128]{2,1,0:T(8,128)(2,1)S(1)}, bf16[2,512,128]{2,1,0:T(8,128)(2,1)S(1)}, u32[]{:S(2)}, u32[]{:S(2)}) %collective-permute-start.10) | collective-permute-done | bytes 262176 | tf_op jit(solution)/shard_map/ppermute | solution.py:240
  13.8 1.5 %collective-permute-start.1 = (bf16[2,512,128]{2,1,0:T(8,128)(2,1)S(1)}, bf16[2,512,128]{2,1,0:T(8,128)(2,1)S(1)}, u32[]{:S(2)}, u32[]{:S(2)}) collective-permute-start(bf16[2,512,128]{2,1,0:T(8,128)(2,1)S(1)} %pad_maximum_fusion.refs_2_), channel_id=1, source_target_pairs={{0,4},{4,8},{8,12},{12,16},{16,20},{20,24},{24,28},{28,0},{1,5},{5... | collective-permute-start | bytes 786440 | tf_op jit(solution)/shard_map/ppermute | solution.py:240
  15.3 5.0 %collective-permute-done.7.refs_0_ = bf16[2,512,128]{2,1,0:T(8,128)(2,1)S(1)} collective-permute-done((bf16[2,512,128]{2,1,0:T(8,128)(2,1)S(1)}, bf16[2,512,128]{2,1,0:T(8,128)(2,1)S(1)}, u32[]{:S(2)}, u32[]{:S(2)}) %collective-permute-start.7) | collective-permute-done | bytes 262176 | tf_op jit(solution)/shard_map/ppermute | solution.py:240
  20.4 3.0 %collective-permute-start.2 = (bf16[2,512,128]{2,1,0:T(8,128)(2,1)S(1)}, bf16[2,512,128]{2,1,0:T(8,128)(2,1)S(1)}, u32[]{:S(2)}, u32[]{:S(2)}) collective-permute-start(bf16[2,512,128]{2,1,0:T(8,128)(2,1)S(1)} %pad_maximum_fusion.refs_2_), channel_id=1, source_target_pairs={{0,28},{4,0},{8,4},{12,8},{16,12},{20,16},{24,20},{28,24},{1,29},{... | collective-permute-start | bytes 786440 | tf_op jit(solution)/shard_map/ppermute | solution.py:240
  23.3 3.8 %collective-permute-done.8.refs_1_ = bf16[2,512,128]{2,1,0:T(8,128)(2,1)} collective-permute-done((bf16[2,512,128]{2,1,0:T(8,128)(2,1)S(1)}, bf16[2,512,128]{2,1,0:T(8,128)(2,1)}, u32[]{:S(2)}, u32[]{:S(2)}) %collective-permute-start.8) | collective-permute-done | bytes 262176 | tf_op jit(solution)/shard_map/ppermute | solution.py:240
  27.1 2.0 %collective-permute-start.3 = (bf16[2,512,128]{2,1,0:T(8,128)(2,1)S(1)}, bf16[2,512,128]{2,1,0:T(8,128)(2,1)S(1)}, u32[]{:S(2)}, u32[]{:S(2)}) collective-permute-start(bf16[2,512,128]{2,1,0:T(8,128)(2,1)S(1)} %pad_maximum_fusion.refs_2_), channel_id=1, source_target_pairs={{0,24},{4,28},{8,0},{12,4},{16,8},{20,12},{24,16},{28,20},{1,25},{... | collective-permute-start | bytes 786440 | tf_op jit(solution)/shard_map/ppermute | solution.py:240
  29.1 0.1 pad_add_fusion.me_ref
  29.2 0.0 collective-permute-done.9.refs_3_
  29.2 0.6 copy-done.2
  29.8 9.1 %shard_map.86 = (bf16[128,512]{1,0:T(8,128)(2,1)S(1)}, bf16[128,512]{1,0:T(8,128)(2,1)S(1)}, bf16[128,512]{1,0:T(8,128)(2,1)S(1)}, bf16[128,512]{1,0:T(8,128)(2,...) custom-call(s32[4,8]{1,0:T(4,128)S(1)} %copy-done.2, ...), custom_call_target="tpu_custom_call" | custom-call | flops 2000000000 | bytes 20000000 | tf_op jit(solution)/shard_map/pallas_call | solution.py:140
  38.9 0.1 collective-permute-start.21
  38.9 0.0 collective-permute-done.refs_0_
  39.0 0.1 collective-permute-start.22
  39.0 0.0 collective-permute-done.1.refs_1_
  39.0 2.0 %collective-permute-start.23 = (bf16[2,512,128]{2,1,0:T(8,128)(2,1)S(1)}, bf16[2,512,128]{2,1,0:T(8,128)(2,1)S(1)}, u32[]{:S(2)}, u32[]{:S(2)}) collective-permute-start(bf16[2,512,128]{2,1,0:T(8,128)(2,1)S(1)} %get-tuple-element.49), channel_id=1, source_target_pairs={{0,4},{4,8},{8,12},{12,16},{16,20},{20,24},{24,28},{28,0},{1,5},{5... | collective-permute-start | bytes 786440 | tf_op jit(solution)/shard_map/ppermute | solution.py:240
  41.0 0.0 collective-permute-done.2.refs_3_
  41.0 0.0 collective-permute-start.11
  41.0 0.9 collective-permute-done.3.refs_4_
  41.9 1.5 %collective-permute-start.12 = (bf16[128,512]{1,0:T(8,128)(2,1)S(1)}, bf16[128,512]{1,0:T(8,128)(2,1)S(1)}, u32[]{:S(2)}, u32[]{:S(2)}) collective-permute-start(bf16[128,512]{1,0:T(8,128)(2,1)S(1)} %get-tuple-element.35), channel_id=1, source_target_pairs={{0,2},{1,3},{2,0},{3,1},{4,6},{5,7},{6,4},{7,5},{8,10},{9,11},{10,... | collective-permute-start | bytes 393224 | tf_op jit(solution)/shard_map/ppermute | solution.py:245
  43.4 8.4 %shard_map.85 = (bf16[128,512]{1,0:T(8,128)(2,1)S(1)}, bf16[128,512]{1,0:T(8,128)(2,1)S(1)}, bf16[128,512]{1,0:T(8,128)(2,1)S(1)}, bf16[128,512]{1,0:T(8,128)(2,...) custom-call(s32[4,8]{1,0:T(4,128)S(1)} %copy-done.2, ...), custom_call_target="tpu_custom_call" | custom-call | flops 2000000000 | bytes 20000000 | tf_op jit(solution)/shard_map/pallas_call | solution.py:140
  51.8 0.0 collective-permute-done.11.refs_5_
  51.8 0.5 collective-permute-start.24
  52.3 0.0 collective-permute-done.12.refs_6_
  52.3 3.4 %collective-permute-start.14 = (bf16[2,512,128]{2,1,0:T(8,128)(2,1)S(1)}, bf16[2,512,128]{2,1,0:T(8,128)(2,1)S(1)}, u32[]{:S(2)}, u32[]{:S(2)}) collective-permute-start(bf16[2,512,128]{2,1,0:T(8,128)(2,1)S(1)} %get-tuple-element.37), channel_id=1, source_target_pairs={{0,24},{4,28},{8,0},{12,4},{16,8},{20,12},{24,16},{28,20},{1,25},{... | collective-permute-start | bytes 786440 | tf_op jit(solution)/shard_map/ppermute | solution.py:240
  55.7 0.0 collective-permute-done.21.refs_0_
  55.7 2.7 %collective-permute-start.15 = (bf16[2,512,128]{2,1,0:T(8,128)(2,1)S(1)}, bf16[2,512,128]{2,1,0:T(8,128)(2,1)S(1)}, u32[]{:S(2)}, u32[]{:S(2)}) collective-permute-start(bf16[2,512,128]{2,1,0:T(8,128)(2,1)S(1)} %get-tuple-element.38), channel_id=1, source_target_pairs={{0,28},{4,0},{8,4},{12,8},{16,12},{20,16},{24,20},{28,24},{1,29},{... | collective-permute-start | bytes 786440 | tf_op jit(solution)/shard_map/ppermute | solution.py:240
  58.4 0.0 collective-permute-done.22.refs_1_
  58.4 0.0 collective-permute-start.16
  58.4 0.0 collective-permute-done.23.refs_3_
  58.4 1.0 %collective-permute-start.17 = (bf16[2,512,128]{2,1,0:T(8,128)(2,1)S(1)}, bf16[2,512,128]{2,1,0:T(8,128)(2,1)S(1)}, u32[]{:S(2)}, u32[]{:S(2)}) collective-permute-start(bf16[2,512,128]{2,1,0:T(8,128)(2,1)S(1)} %get-tuple-element.41), channel_id=1, source_target_pairs={{0,8},{4,12},{8,16},{12,20},{16,24},{20,28},{24,0},{28,4},{1,9},{5... | collective-permute-start | bytes 786440 | tf_op jit(solution)/shard_map/ppermute | solution.py:240
  59.4 3.5 %collective-permute-done.24.refs_4_ = bf16[2,512,128]{2,1,0:T(8,128)(2,1)S(1)} collective-permute-done((bf16[2,512,128]{2,1,0:T(8,128)(2,1)S(1)}, bf16[2,512,128]{2,1,0:T(8,128)(2,1)S(1)}, u32[]{:S(2)}, u32[]{:S(2)}) %collective-permute-start.24) | collective-permute-done | bytes 262176 | tf_op jit(solution)/shard_map/ppermute | solution.py:240
  62.9 0.0 collective-permute-start.13
  62.9 4.1 %collective-permute-done.14.refs_0_ = bf16[2,512,128]{2,1,0:T(8,128)(2,1)S(1)} collective-permute-done((bf16[2,512,128]{2,1,0:T(8,128)(2,1)S(1)}, bf16[2,512,128]{2,1,0:T(8,128)(2,1)S(1)}, u32[]{:S(2)}, u32[]{:S(2)}) %collective-permute-start.14) | collective-permute-done | bytes 262176 | tf_op jit(solution)/shard_map/ppermute | solution.py:240
  67.0 0.0 collective-permute-start.4
  67.0 3.3 %collective-permute-done.15.refs_1_ = bf16[2,512,128]{2,1,0:T(8,128)(2,1)S(1)} collective-permute-done((bf16[2,512,128]{2,1,0:T(8,128)(2,1)S(1)}, bf16[2,512,128]{2,1,0:T(8,128)(2,1)S(1)}, u32[]{:S(2)}, u32[]{:S(2)}) %collective-permute-start.15) | collective-permute-done | bytes 262176 | tf_op jit(solution)/shard_map/ppermute | solution.py:240
  70.2 0.6 collective-permute-start.5
  70.9 4.9 %collective-permute-done.16.refs_3_ = bf16[2,512,128]{2,1,0:T(8,128)(2,1)S(1)} collective-permute-done((bf16[2,512,128]{2,1,0:T(8,128)(2,1)S(1)}, bf16[2,512,128]{2,1,0:T(8,128)(2,1)S(1)}, u32[]{:S(2)}, u32[]{:S(2)}) %collective-permute-start.16) | collective-permute-done | bytes 262176 | tf_op jit(solution)/shard_map/ppermute | solution.py:240
  75.8 0.0 collective-permute-start.6
  75.8 0.7 shard_map.88
  76.5 1.6 %collective-permute-done.17.refs_4_ = bf16[2,512,128]{2,1,0:T(8,128)(2,1)S(1)} collective-permute-done((bf16[2,512,128]{2,1,0:T(8,128)(2,1)S(1)}, bf16[2,512,128]{2,1,0:T(8,128)(2,1)S(1)}, u32[]{:S(2)}, u32[]{:S(2)}) %collective-permute-start.17) | collective-permute-done | bytes 262176 | tf_op jit(solution)/shard_map/ppermute | solution.py:240
  78.1 0.0 collective-permute-start.25
  78.1 0.7 shard_map.87
  78.8 0.0 collective-permute-done.13.refs_7_
  78.9 0.6 collective-permute-start.26
  79.5 0.0 collective-permute-done.4.refs_1_
  79.5 1.3 %collective-permute-start.27 = (bf16[2,128,128]{2,1,0:T(8,128)(2,1)S(1)}, bf16[2,128,128]{2,1,0:T(8,128)(2,1)S(1)}, u32[]{:S(2)}, u32[]{:S(2)}) collective-permute-start(bf16[2,128,128]{2,1,0:T(8,128)(2,1)S(1)} %get-tuple-element.54), channel_id=1, source_target_pairs={{0,3},{1,2},{2,1},{3,0},{4,7},{5,6},{6,5},{7,4},{8,11},{9,10},{10,... | collective-permute-start | bytes 196616 | tf_op jit(solution)/shard_map/ppermute | solution.py:245
  80.8 0.0 collective-permute-done.5.refs_2_
  80.8 0.3 collective-permute-start.18
  81.1 0.0 collective-permute-done.6.refs_3_
  81.1 1.0 %collective-permute-start.19 = (bf16[2,128,128]{2,1,0:T(8,128)(2,1)S(1)}, bf16[2,128,128]{2,1,0:T(8,128)(2,1)S(1)}, u32[]{:S(2)}, u32[]{:S(2)}) collective-permute-start(bf16[2,128,128]{2,1,0:T(8,128)(2,1)S(1)} %get-tuple-element.44), channel_id=1, source_target_pairs={{0,2},{1,3},{2,0},{3,1},{4,6},{5,7},{6,4},{7,5},{8,10},{9,11},{10,... | collective-permute-start | bytes 196616 | tf_op jit(solution)/shard_map/ppermute | solution.py:245
  82.1 0.0 collective-permute-done.25.refs_13_
  82.1 0.6 collective-permute-start.20
  82.7 1.2 %collective-permute-done.26.refs_14_ = bf16[2,128,128]{2,1,0:T(8,128)(2,1)S(1)} collective-permute-done((bf16[2,128,128]{2,1,0:T(8,128)(2,1)S(1)}, bf16[2,128,128]{2,1,0:T(8,128)(2,1)S(1)}, u32[]{:S(2)}, u32[]{:S(2)}) %collective-permute-start.26) | collective-permute-done | bytes 65568 | tf_op jit(solution)/shard_map/ppermute | solution.py:245
  83.8 0.6 collective-permute-done.27.refs_15_
  84.4 0.0 collective-permute-done.18.refs_9_
  84.4 2.2 %collective-permute-done.19.refs_10_ = bf16[2,128,128]{2,1,0:T(8,128)(2,1)S(1)} collective-permute-done((bf16[2,128,128]{2,1,0:T(8,128)(2,1)S(1)}, bf16[2,128,128]{2,1,0:T(8,128)(2,1)S(1)}, u32[]{:S(2)}, u32[]{:S(2)}) %collective-permute-start.19) | collective-permute-done | bytes 65568 | tf_op jit(solution)/shard_map/ppermute | solution.py:245
  86.6 0.6 collective-permute-done.20.refs_11_
  87.3 1.9 %shard_map.89 = (bf16[128,4096]{1,0:T(8,128)(2,1)}, bf16[128,1024]{1,0:T(8,128)(2,1)}, bf16[128,1024]{1,0:T(8,128)(2,1)}) custom-call(s32[2]{0:T(128)S(1)} %pad_add_fusion.me_ref, bf16[128,512]{1,0:T(8,128)(2,1)S(1)} %get-tuple-element.29.refs_0_, bf16[128,512]{1,0:T(8,128)(2,1)S(1)} %collective-permute-done.4.refs_1_, ...), custom_call_target="tpu_custom_call" | custom-call | tf_op jit(solution)/shard_map/pallas_call | solution.py:224
  (9 shorter events, 0.1 us)
Async XLA Ops:
  0.6 28.5 %copy-start = (bf16[512,1024]{1,0:T(8,128)(2,1)S(1)}, bf16[512,1024]{1,0:T(8,128)(2,1)}, u32[]{:S(2)}) copy-start(bf16[512,1024]{1,0:T(8,128)(2,1)} %queries_hbm.3) | copy-start | bytes 3145732
  0.6 28.5 %copy-start.1 = (bf16[512,1024]{1,0:T(8,128)(2,1)S(1)}, bf16[512,1024]{1,0:T(8,128)(2,1)}, u32[]{:S(2)}) copy-start(bf16[512,1024]{1,0:T(8,128)(2,1)} %outgrad_hbm.3) | copy-start | bytes 3145732
  2.0 11.8 %collective-permute-start.10 = (bf16[2,512,128]{2,1,0:T(8,128)(2,1)S(1)}, bf16[2,512,128]{2,1,0:T(8,128)(2,1)S(1)}, u32[]{:S(2)}, u32[]{:S(2)}) collective-permute-start(bf16[2,512,128]{2,1,0:T(8,128)(2,1)S(1)} %pad_maximum_fusion.1.refs_2_), channel_id=1, source_target_pairs={{0,24},{4,28},{8,0},{12,4},{16,8},{20,12},{24,16},{28,20},{1,25},{... | collective-permute-start | bytes 786440 | tf_op jit(solution)/shard_map/ppermute | solution.py:240
  7.1 13.3 %collective-permute-start.7 = (bf16[2,512,128]{2,1,0:T(8,128)(2,1)S(1)}, bf16[2,512,128]{2,1,0:T(8,128)(2,1)S(1)}, u32[]{:S(2)}, u32[]{:S(2)}) collective-permute-start(bf16[2,512,128]{2,1,0:T(8,128)(2,1)S(1)} %pad_maximum_fusion.1.refs_2_), channel_id=1, source_target_pairs={{0,8},{4,12},{8,16},{12,20},{16,24},{20,28},{24,0},{28,4},{1,9},{5... | collective-permute-start | bytes 786440 | tf_op jit(solution)/shard_map/ppermute | solution.py:240
  7.1 20.1 %collective-permute-start.8 = (bf16[2,512,128]{2,1,0:T(8,128)(2,1)S(1)}, bf16[2,512,128]{2,1,0:T(8,128)(2,1)}, u32[]{:S(2)}, u32[]{:S(2)}) collective-permute-start(bf16[2,512,128]{2,1,0:T(8,128)(2,1)S(1)} %pad_maximum_fusion.1.refs_2_), channel_id=1, source_target_pairs={{0,4},{4,8},{8,12},{12,16},{16,20},{20,24},{24,28},{28,0},{1,5},{5... | collective-permute-start | bytes 786440 | tf_op jit(solution)/shard_map/ppermute | solution.py:240
  8.6 20.6 %collective-permute-start.9 = (bf16[2,512,128]{2,1,0:T(8,128)(2,1)S(1)}, bf16[2,512,128]{2,1,0:T(8,128)(2,1)}, u32[]{:S(2)}, u32[]{:S(2)}) collective-permute-start(bf16[2,512,128]{2,1,0:T(8,128)(2,1)S(1)} %pad_maximum_fusion.1.refs_2_), channel_id=1, source_target_pairs={{0,28},{4,0},{8,4},{12,8},{16,12},{20,16},{24,20},{28,24},{1,29},{... | collective-permute-start | bytes 786440 | tf_op jit(solution)/shard_map/ppermute | solution.py:240
  11.9 27.1 %collective-permute-start = (bf16[2,512,128]{2,1,0:T(8,128)(2,1)S(1)}, bf16[2,512,128]{2,1,0:T(8,128)(2,1)S(1)}, u32[]{:S(2)}, u32[]{:S(2)}) collective-permute-start(bf16[2,512,128]{2,1,0:T(8,128)(2,1)S(1)} %pad_maximum_fusion.refs_2_), channel_id=1, source_target_pairs={{0,8},{4,12},{8,16},{12,20},{16,24},{20,28},{24,0},{28,4},{1,9},{5... | collective-permute-start | bytes 786440 | tf_op jit(solution)/shard_map/ppermute | solution.py:240
  13.8 25.2 %collective-permute-start.1 = (bf16[2,512,128]{2,1,0:T(8,128)(2,1)S(1)}, bf16[2,512,128]{2,1,0:T(8,128)(2,1)S(1)}, u32[]{:S(2)}, u32[]{:S(2)}) collective-permute-start(bf16[2,512,128]{2,1,0:T(8,128)(2,1)S(1)} %pad_maximum_fusion.refs_2_), channel_id=1, source_target_pairs={{0,4},{4,8},{8,12},{12,16},{16,20},{20,24},{24,28},{28,0},{1,5},{5... | collective-permute-start | bytes 786440 | tf_op jit(solution)/shard_map/ppermute | solution.py:240
  20.4 20.7 %collective-permute-start.2 = (bf16[2,512,128]{2,1,0:T(8,128)(2,1)S(1)}, bf16[2,512,128]{2,1,0:T(8,128)(2,1)S(1)}, u32[]{:S(2)}, u32[]{:S(2)}) collective-permute-start(bf16[2,512,128]{2,1,0:T(8,128)(2,1)S(1)} %pad_maximum_fusion.refs_2_), channel_id=1, source_target_pairs={{0,28},{4,0},{8,4},{12,8},{16,12},{20,16},{24,20},{28,24},{1,29},{... | collective-permute-start | bytes 786440 | tf_op jit(solution)/shard_map/ppermute | solution.py:240
  27.1 14.8 %collective-permute-start.3 = (bf16[2,512,128]{2,1,0:T(8,128)(2,1)S(1)}, bf16[2,512,128]{2,1,0:T(8,128)(2,1)S(1)}, u32[]{:S(2)}, u32[]{:S(2)}) collective-permute-start(bf16[2,512,128]{2,1,0:T(8,128)(2,1)S(1)} %pad_maximum_fusion.refs_2_), channel_id=1, source_target_pairs={{0,24},{4,28},{8,0},{12,4},{16,8},{20,12},{24,16},{28,20},{1,25},{... | collective-permute-start | bytes 786440 | tf_op jit(solution)/shard_map/ppermute | solution.py:240
  29.1 0.7 copy-start.2
  29.1 0.7 copy-start.3
  38.9 16.8 %collective-permute-start.21 = (bf16[2,512,128]{2,1,0:T(8,128)(2,1)S(1)}, bf16[2,512,128]{2,1,0:T(8,128)(2,1)S(1)}, u32[]{:S(2)}, u32[]{:S(2)}) collective-permute-start(bf16[2,512,128]{2,1,0:T(8,128)(2,1)S(1)} %get-tuple-element.46), channel_id=1, source_target_pairs={{0,24},{4,28},{8,0},{12,4},{16,8},{20,12},{24,16},{28,20},{1,25},{... | collective-permute-start | bytes 786440 | tf_op jit(solution)/shard_map/ppermute | solution.py:240
  39.0 19.4 %collective-permute-start.22 = (bf16[2,512,128]{2,1,0:T(8,128)(2,1)S(1)}, bf16[2,512,128]{2,1,0:T(8,128)(2,1)S(1)}, u32[]{:S(2)}, u32[]{:S(2)}) collective-permute-start(bf16[2,512,128]{2,1,0:T(8,128)(2,1)S(1)} %get-tuple-element.47), channel_id=1, source_target_pairs={{0,28},{4,0},{8,4},{12,8},{16,12},{20,16},{24,20},{28,24},{1,29},{... | collective-permute-start | bytes 786440 | tf_op jit(solution)/shard_map/ppermute | solution.py:240
  39.0 19.3 %collective-permute-start.23 = (bf16[2,512,128]{2,1,0:T(8,128)(2,1)S(1)}, bf16[2,512,128]{2,1,0:T(8,128)(2,1)S(1)}, u32[]{:S(2)}, u32[]{:S(2)}) collective-permute-start(bf16[2,512,128]{2,1,0:T(8,128)(2,1)S(1)} %get-tuple-element.49), channel_id=1, source_target_pairs={{0,4},{4,8},{8,12},{12,16},{16,20},{20,24},{24,28},{28,0},{1,5},{5... | collective-permute-start | bytes 786440 | tf_op jit(solution)/shard_map/ppermute | solution.py:240
  41.0 10.7 %collective-permute-start.11 = (bf16[128,512]{1,0:T(8,128)(2,1)S(1)}, bf16[128,512]{1,0:T(8,128)(2,1)S(1)}, u32[]{:S(2)}, u32[]{:S(2)}) collective-permute-start(bf16[128,512]{1,0:T(8,128)(2,1)S(1)} %get-tuple-element.34), channel_id=1, source_target_pairs={{0,1},{1,0},{2,3},{3,2},{4,5},{5,4},{6,7},{7,6},{8,9},{9,8},{10,11... | collective-permute-start | bytes 393224 | tf_op jit(solution)/shard_map/ppermute | solution.py:245
  41.9 10.4 %collective-permute-start.12 = (bf16[128,512]{1,0:T(8,128)(2,1)S(1)}, bf16[128,512]{1,0:T(8,128)(2,1)S(1)}, u32[]{:S(2)}, u32[]{:S(2)}) collective-permute-start(bf16[128,512]{1,0:T(8,128)(2,1)S(1)} %get-tuple-element.35), channel_id=1, source_target_pairs={{0,2},{1,3},{2,0},{3,1},{4,6},{5,7},{6,4},{7,5},{8,10},{9,11},{10,... | collective-permute-start | bytes 393224 | tf_op jit(solution)/shard_map/ppermute | solution.py:245
  51.8 11.1 %collective-permute-start.24 = (bf16[2,512,128]{2,1,0:T(8,128)(2,1)S(1)}, bf16[2,512,128]{2,1,0:T(8,128)(2,1)S(1)}, u32[]{:S(2)}, u32[]{:S(2)}) collective-permute-start(bf16[2,512,128]{2,1,0:T(8,128)(2,1)S(1)} %get-tuple-element.50), channel_id=1, source_target_pairs={{0,8},{4,12},{8,16},{12,20},{16,24},{20,28},{24,0},{28,4},{1,9},{5... | collective-permute-start | bytes 786440 | tf_op jit(solution)/shard_map/ppermute | solution.py:240
  52.3 14.7 %collective-permute-start.14 = (bf16[2,512,128]{2,1,0:T(8,128)(2,1)S(1)}, bf16[2,512,128]{2,1,0:T(8,128)(2,1)S(1)}, u32[]{:S(2)}, u32[]{:S(2)}) collective-permute-start(bf16[2,512,128]{2,1,0:T(8,128)(2,1)S(1)} %get-tuple-element.37), channel_id=1, source_target_pairs={{0,24},{4,28},{8,0},{12,4},{16,8},{20,12},{24,16},{28,20},{1,25},{... | collective-permute-start | bytes 786440 | tf_op jit(solution)/shard_map/ppermute | solution.py:240
  55.7 14.5 %collective-permute-start.15 = (bf16[2,512,128]{2,1,0:T(8,128)(2,1)S(1)}, bf16[2,512,128]{2,1,0:T(8,128)(2,1)S(1)}, u32[]{:S(2)}, u32[]{:S(2)}) collective-permute-start(bf16[2,512,128]{2,1,0:T(8,128)(2,1)S(1)} %get-tuple-element.38), channel_id=1, source_target_pairs={{0,28},{4,0},{8,4},{12,8},{16,12},{20,16},{24,20},{28,24},{1,29},{... | collective-permute-start | bytes 786440 | tf_op jit(solution)/shard_map/ppermute | solution.py:240
  58.4 17.4 %collective-permute-start.16 = (bf16[2,512,128]{2,1,0:T(8,128)(2,1)S(1)}, bf16[2,512,128]{2,1,0:T(8,128)(2,1)S(1)}, u32[]{:S(2)}, u32[]{:S(2)}) collective-permute-start(bf16[2,512,128]{2,1,0:T(8,128)(2,1)S(1)} %get-tuple-element.40), channel_id=1, source_target_pairs={{0,4},{4,8},{8,12},{12,16},{16,20},{20,24},{24,28},{28,0},{1,5},{5... | collective-permute-start | bytes 786440 | tf_op jit(solution)/shard_map/ppermute | solution.py:240
  58.4 19.7 %collective-permute-start.17 = (bf16[2,512,128]{2,1,0:T(8,128)(2,1)S(1)}, bf16[2,512,128]{2,1,0:T(8,128)(2,1)S(1)}, u32[]{:S(2)}, u32[]{:S(2)}) collective-permute-start(bf16[2,512,128]{2,1,0:T(8,128)(2,1)S(1)} %get-tuple-element.41), channel_id=1, source_target_pairs={{0,8},{4,12},{8,16},{12,20},{16,24},{20,28},{24,0},{28,4},{1,9},{5... | collective-permute-start | bytes 786440 | tf_op jit(solution)/shard_map/ppermute | solution.py:240
  62.9 15.9 %collective-permute-start.13 = (bf16[128,512]{1,0:T(8,128)(2,1)S(1)}, bf16[128,512]{1,0:T(8,128)(2,1)S(1)}, u32[]{:S(2)}, u32[]{:S(2)}) collective-permute-start(bf16[128,512]{1,0:T(8,128)(2,1)S(1)} %get-tuple-element.36), channel_id=1, source_target_pairs={{0,3},{1,2},{2,1},{3,0},{4,7},{5,6},{6,5},{7,4},{8,11},{9,10},{10,... | collective-permute-start | bytes 393224 | tf_op jit(solution)/shard_map/ppermute | solution.py:245
  67.0 12.5 %collective-permute-start.4 = (bf16[128,512]{1,0:T(8,128)(2,1)S(1)}, bf16[128,512]{1,0:T(8,128)(2,1)S(1)}, u32[]{:S(2)}, u32[]{:S(2)}) collective-permute-start(bf16[128,512]{1,0:T(8,128)(2,1)S(1)} %get-tuple-element.30), channel_id=1, source_target_pairs={{0,1},{1,0},{2,3},{3,2},{4,5},{5,4},{6,7},{7,6},{8,9},{9,8},{10,11... | collective-permute-start | bytes 393224 | tf_op jit(solution)/shard_map/ppermute | solution.py:245
  70.2 10.6 %collective-permute-start.5 = (bf16[128,512]{1,0:T(8,128)(2,1)S(1)}, bf16[128,512]{1,0:T(8,128)(2,1)S(1)}, u32[]{:S(2)}, u32[]{:S(2)}) collective-permute-start(bf16[128,512]{1,0:T(8,128)(2,1)S(1)} %get-tuple-element.31), channel_id=1, source_target_pairs={{0,2},{1,3},{2,0},{3,1},{4,6},{5,7},{6,4},{7,5},{8,10},{9,11},{10,... | collective-permute-start | bytes 393224 | tf_op jit(solution)/shard_map/ppermute | solution.py:245
  75.8 5.3 %collective-permute-start.6 = (bf16[128,512]{1,0:T(8,128)(2,1)S(1)}, bf16[128,512]{1,0:T(8,128)(2,1)S(1)}, u32[]{:S(2)}, u32[]{:S(2)}) collective-permute-start(bf16[128,512]{1,0:T(8,128)(2,1)S(1)} %get-tuple-element.32), channel_id=1, source_target_pairs={{0,3},{1,2},{2,1},{3,0},{4,7},{5,6},{6,5},{7,4},{8,11},{9,10},{10,... | collective-permute-start | bytes 393224 | tf_op jit(solution)/shard_map/ppermute | solution.py:245
  78.1 3.9 %collective-permute-start.25 = (bf16[2,128,128]{2,1,0:T(8,128)(2,1)S(1)}, bf16[2,128,128]{2,1,0:T(8,128)(2,1)S(1)}, u32[]{:S(2)}, u32[]{:S(2)}) collective-permute-start(bf16[2,128,128]{2,1,0:T(8,128)(2,1)S(1)} %get-tuple-element.52), channel_id=1, source_target_pairs={{0,1},{1,0},{2,3},{3,2},{4,5},{5,4},{6,7},{7,6},{8,9},{9,8},{10,11... | collective-permute-start | bytes 196616 | tf_op jit(solution)/shard_map/ppermute | solution.py:245
  78.9 5.0 %collective-permute-start.26 = (bf16[2,128,128]{2,1,0:T(8,128)(2,1)S(1)}, bf16[2,128,128]{2,1,0:T(8,128)(2,1)S(1)}, u32[]{:S(2)}, u32[]{:S(2)}) collective-permute-start(bf16[2,128,128]{2,1,0:T(8,128)(2,1)S(1)} %get-tuple-element.53), channel_id=1, source_target_pairs={{0,2},{1,3},{2,0},{3,1},{4,6},{5,7},{6,4},{7,5},{8,10},{9,11},{10,... | collective-permute-start | bytes 196616 | tf_op jit(solution)/shard_map/ppermute | solution.py:245
  79.5 4.9 %collective-permute-start.27 = (bf16[2,128,128]{2,1,0:T(8,128)(2,1)S(1)}, bf16[2,128,128]{2,1,0:T(8,128)(2,1)S(1)}, u32[]{:S(2)}, u32[]{:S(2)}) collective-permute-start(bf16[2,128,128]{2,1,0:T(8,128)(2,1)S(1)} %get-tuple-element.54), channel_id=1, source_target_pairs={{0,3},{1,2},{2,1},{3,0},{4,7},{5,6},{6,5},{7,4},{8,11},{9,10},{10,... | collective-permute-start | bytes 196616 | tf_op jit(solution)/shard_map/ppermute | solution.py:245
  80.8 3.7 %collective-permute-start.18 = (bf16[2,128,128]{2,1,0:T(8,128)(2,1)S(1)}, bf16[2,128,128]{2,1,0:T(8,128)(2,1)S(1)}, u32[]{:S(2)}, u32[]{:S(2)}) collective-permute-start(bf16[2,128,128]{2,1,0:T(8,128)(2,1)S(1)} %get-tuple-element.43), channel_id=1, source_target_pairs={{0,1},{1,0},{2,3},{3,2},{4,5},{5,4},{6,7},{7,6},{8,9},{9,8},{10,11... | collective-permute-start | bytes 196616 | tf_op jit(solution)/shard_map/ppermute | solution.py:245
  81.1 5.5 %collective-permute-start.19 = (bf16[2,128,128]{2,1,0:T(8,128)(2,1)S(1)}, bf16[2,128,128]{2,1,0:T(8,128)(2,1)S(1)}, u32[]{:S(2)}, u32[]{:S(2)}) collective-permute-start(bf16[2,128,128]{2,1,0:T(8,128)(2,1)S(1)} %get-tuple-element.44), channel_id=1, source_target_pairs={{0,2},{1,3},{2,0},{3,1},{4,6},{5,7},{6,4},{7,5},{8,10},{9,11},{10,... | collective-permute-start | bytes 196616 | tf_op jit(solution)/shard_map/ppermute | solution.py:245
  82.1 5.2 %collective-permute-start.20 = (bf16[2,128,128]{2,1,0:T(8,128)(2,1)S(1)}, bf16[2,128,128]{2,1,0:T(8,128)(2,1)S(1)}, u32[]{:S(2)}, u32[]{:S(2)}) collective-permute-start(bf16[2,128,128]{2,1,0:T(8,128)(2,1)S(1)} %get-tuple-element.45), channel_id=1, source_target_pairs={{0,3},{1,2},{2,1},{3,0},{4,7},{5,6},{6,5},{7,4},{8,11},{9,10},{10,... | collective-permute-start | bytes 196616 | tf_op jit(solution)/shard_map/ppermute | solution.py:245

commit v3 on v2

v3 whole, which is shorter than its diff:
```python
import functools
import math

import jax
import jax.numpy as jnp
from jax import lax
from jax.experimental import pallas as pl
from jax.experimental.pallas import tpu as pltpu
from jax.sharding import PartitionSpec as P

HEAD_SIZE = 128
BLOCK_TOKENS = 128
SLOTS = 8
REACH = 2
SHARDS = 2 * REACH + 1
F32 = jnp.float32
BF16 = jnp.bfloat16
ROWS_BY_ROWS = (((1,), (1,)), ((), ()))
COLS_BY_COLS = (((0,), (0,)), ((), ()))
MIB = 2**20

VMEM = pl.BlockSpec(memory_space=pltpu.VMEM)
SMEM = pl.BlockSpec(memory_space=pltpu.SMEM)
HBM = pl.BlockSpec(memory_space=pltpu.HBM)
ANY = pl.BlockSpec(memory_space=pl.ANY)

BEHIND, CROSS, OWN, OTHER, AHEAD = range(SHARDS)


def attention_kernel(cycle_blocks, places_out, *refs):
    blocks_ref, counts_ref, me_ref, queries, outgrad = refs[:5]
    refs = refs[5:]
    window_hbm, refs = refs[:SHARDS], refs[SHARDS:]
    dqueries_refs, refs = refs[:places_out], refs[places_out:]
    outs, refs = refs[:SHARDS], refs[SHARDS:]
    window, sums, scores_ref, dprobs_ref = refs[:4]
    block_keys, block_values, dqueries_ref, sems = refs[4:]
    tokens, query_width = dqueries_ref.shape
    group = query_width // HEAD_SIZE
    own_blocks, rows = tokens // BLOCK_TOKENS, group * BLOCK_TOKENS
    scale = 1.0 / math.sqrt(HEAD_SIZE)
    scale_log2 = scale * math.log2(math.e)

    copies = []
    for j in range(SHARDS):
        place = window.at[:, pl.ds(j * tokens, tokens), :]
        copies.append(pltpu.make_async_copy(window_hbm[j], place, sems.at[j]))
    for copy in copies:
        copy.start()
    sums[...] = jnp.zeros_like(sums)
    for copy in copies:
        copy.wait()
    half = cycle_blocks // 2
    me_block = me_ref[0] * own_blocks
    mirrored = me_ref[0] % 2 == 1

    def query_block(qblock, live):
        row_ds = pl.ds(pl.multiple_of(qblock * BLOCK_TOKENS, BLOCK_TOKENS), BLOCK_TOKENS)
        q_cols = [slice(g * HEAD_SIZE, (g + 1) * HEAD_SIZE) for g in range(group)]
        slots = [slice(s * BLOCK_TOKENS, (s + 1) * BLOCK_TOKENS) for s in range(live)]
        places = []
        for s in range(live):
            ahead = lax.rem(blocks_ref[qblock, s] - me_block + half + cycle_blocks, cycle_blocks)
            place = ahead - half + REACH * own_blocks
            shard = lax.div(place, own_blocks)
            flipped = place + (2 * REACH - 2 * shard) * own_blocks
            place = jnp.where(mirrored, flipped, place)
            place = pl.ds(pl.multiple_of(place * BLOCK_TOKENS, BLOCK_TOKENS), BLOCK_TOKENS)
            places.append(place)
            block_keys[slots[s]] = window[0, place]
            block_values[slots[s]] = window[1, place]
        q_ds = pl.ds(pl.multiple_of(qblock * rows, rows), rows)
        q, o = queries[q_ds], outgrad[q_ds]

        def fold(x, op):
            return op(x.reshape(BLOCK_TOKENS // 8, 8, rows), axis=0)

        top = None
        for s in range(live):
            scores = lax.dot_general(
                block_keys[slots[s]], q, ROWS_BY_ROWS, preferred_element_type=F32
            )
            scores_ref[slots[s]] = scores
            part = fold(scores, jnp.max)
            top = part if s == 0 else jnp.maximum(top, part)
        row_max = jnp.max(top, axis=0, keepdims=True) * scale_log2
        total = weighted = None
        for s in range(live):
            dprobs = lax.dot_general(
                block_values[slots[s]], o, ROWS_BY_ROWS, preferred_element_type=F32
            )
            weights = jnp.exp2(scores_ref[slots[s]] * scale_log2 - row_max)
            dprobs_ref[slots[s]] = dprobs
            scores_ref[slots[s]] = weights
            part, wpart = fold(weights, jnp.sum), fold(weights * dprobs, jnp.sum)
            total = part if s == 0 else total + part
            weighted = wpart if s == 0 else weighted + wpart
        inverse = 1.0 / jnp.sum(total, axis=0, keepdims=True)
        row_delta = jnp.sum(weighted, axis=0, keepdims=True) * inverse
        dq = None
        for s in range(live):
            probs = scores_ref[slots[s]] * inverse
            dscores = (probs * (dprobs_ref[slots[s]] - row_delta)).astype(BF16)
            sums[0, places[s]] += jnp.dot(dscores, q, preferred_element_type=F32)
            sums[1, places[s]] += jnp.dot(probs.astype(BF16), o, preferred_element_type=F32)
            part = lax.dot_general(
                block_keys[slots[s]], dscores, COLS_BY_COLS, preferred_element_type=F32
            )
            dq = part if s == 0 else dq + part
        dq = jnp.transpose(dq * scale).astype(BF16)
        for g in range(group):
            dqueries_ref[row_ds, q_cols[g]] = dq[g * BLOCK_TOKENS : (g + 1) * BLOCK_TOKENS]

    def one_block(qblock, carry):
        for live in range(1, SLOTS + 1):
            pl.when(counts_ref[qblock] == live)(functools.partial(query_block, qblock, live))
        return carry

    lax.fori_loop(0, own_blocks, one_block, 0)
    share = tokens // places_out
    for k in range(places_out):
        first = pl.multiple_of((me_ref[1] ^ k) * share, share)
        dqueries_refs[k][0] = dqueries_ref[pl.ds(first, share)]
    for j, out in enumerate(outs):
        span = slice(j * tokens, (j + 1) * tokens)
        out[0] = (sums[0, span] * scale).astype(BF16)
        out[1] = sums[1, span].astype(BF16)


def attention(cycle_blocks, places_out, scalars, queries, outgrad, window):
    tokens = window[OWN].shape[1]
    query_width = queries.shape[0] // tokens * HEAD_SIZE
    rows = query_width // HEAD_SIZE * BLOCK_TOKENS
    part = (2, tokens, HEAD_SIZE)
    piece = (1, tokens // places_out, query_width)
    shapes = [piece] * places_out + [part] * SHARDS
    keys_rows = SLOTS * BLOCK_TOKENS
    return pl.pallas_call(
        functools.partial(attention_kernel, cycle_blocks, places_out),
        out_shape=[jax.ShapeDtypeStruct(shape, BF16) for shape in shapes],
        in_specs=[SMEM] * 3 + [VMEM] * 2 + [ANY] * SHARDS,
        out_specs=[VMEM] * len(shapes),
        scratch_shapes=[
            pltpu.VMEM((2, SHARDS * tokens, HEAD_SIZE), BF16),
            pltpu.VMEM((2, SHARDS * tokens, HEAD_SIZE), F32),
            pltpu.VMEM((keys_rows, rows), F32),
            pltpu.VMEM((keys_rows, rows), F32),
            pltpu.VMEM((keys_rows, HEAD_SIZE), BF16),
            pltpu.VMEM((keys_rows, HEAD_SIZE), BF16),
            pltpu.VMEM((tokens, query_width), BF16),
            pltpu.SemaphoreType.DMA((SHARDS,)),
        ],
        compiler_params=pltpu.CompilerParams(vmem_limit_bytes=24 * MIB),
        cost_estimate=pl.CostEstimate(
            flops=10**10, bytes_accessed=2 * 10**7, transcendentals=2 * 10**6
        ),
    )(*scalars, queries, outgrad, *window)


def arrange_kernel(heads, queries_hbm, outgrad_hbm, *refs):
    outs, sems = refs[: 2 * heads], refs[2 * heads]
    tokens, query_width = queries_hbm.shape
    group = query_width // heads // HEAD_SIZE
    copies = []
    for head in range(heads):
        for i, source in enumerate((queries_hbm, outgrad_hbm)):
            for block in range(tokens // BLOCK_TOKENS):
                for g in range(group):
                    rows = pl.ds(block * BLOCK_TOKENS, BLOCK_TOKENS)
                    columns = pl.ds((head * group + g) * HEAD_SIZE, HEAD_SIZE)
                    to = pl.ds((block * group + g) * BLOCK_TOKENS, BLOCK_TOKENS)
                    copies.append(
                        pltpu.make_async_copy(
                            source.at[rows, columns],
                            outs[2 * head + i].at[to],
                            sems.at[head, i, block, g],
                        )
                    )
    for copy in copies:
        copy.start()
    for copy in copies:
        copy.wait()


def arrange(heads, queries, outgrad):
    tokens, query_width = queries.shape
    group = query_width // heads // HEAD_SIZE
    out = jax.ShapeDtypeStruct((tokens * group, HEAD_SIZE), BF16)
    outs = pl.pallas_call(
        functools.partial(arrange_kernel, heads),
        out_shape=[out] * (2 * heads),
        in_specs=[HBM] * 2,
        out_specs=[VMEM] * (2 * heads),
        scratch_shapes=[pltpu.SemaphoreType.DMA((heads, 2, tokens // BLOCK_TOKENS, group))],
        compiler_params=pltpu.CompilerParams(vmem_limit_bytes=8 * MIB),
        cost_estimate=pl.CostEstimate(flops=0, bytes_accessed=8 * MIB, transcendentals=0),
    )(queries, outgrad)
    return [outs[2 * head : 2 * head + 2] for head in range(heads)]


def pack_kernel(heads, keys_hbm, values_hbm, *refs):
    outs, sems = refs[:heads], refs[heads]
    copies = []
    for head, out in enumerate(outs):
        columns = pl.ds(head * HEAD_SIZE, HEAD_SIZE)
        for i, source in enumerate((keys_hbm, values_hbm)):
            copies.append(
                pltpu.make_async_copy(source.at[:, columns], out.at[i], sems.at[head, i])
            )
    for copy in copies:
        copy.start()
    for copy in copies:
        copy.wait()


def pack(keys, values):
    heads = keys.shape[1] // HEAD_SIZE
    return pl.pallas_call(
        functools.partial(pack_kernel, heads),
        out_shape=[jax.ShapeDtypeStruct((2, keys.shape[0], HEAD_SIZE), BF16)] * heads,
        in_specs=[HBM] * 2,
        out_specs=[VMEM] * heads,
        scratch_shapes=[pltpu.SemaphoreType.DMA((heads, 2))],
        compiler_params=pltpu.CompilerParams(vmem_limit_bytes=56 * MIB),
    )(keys, values)


def sum_kernel(heads, places_out, me_ref, *refs):
    outs = refs[4 * heads :]
    share = outs[0].shape[2]
    for k, out in enumerate(outs):
        rows = pl.ds(pl.multiple_of((me_ref[1] ^ k) * share, share), share)
        for head in range(heads):
            parts = [part[:, rows].astype(F32) for part in refs[4 * head : 4 * head + 4]]
            out[head] = ((parts[0] + parts[1]) + (parts[2] + parts[3])).astype(BF16)


def sum_parts(me, parts, places_out):
    heads = len(parts) // 4
    _, tokens, width = parts[0].shape
    piece = jax.ShapeDtypeStruct((heads, 2, tokens // places_out, width), BF16)
    return pl.pallas_call(
        functools.partial(sum_kernel, heads, places_out),
        out_shape=[piece] * places_out,
        in_specs=[SMEM] + [VMEM] * len(parts),
        out_specs=[VMEM] * places_out,
        compiler_params=pltpu.CompilerParams(vmem_limit_bytes=8 * MIB),
    )(me, *parts)


def assemble_kernel(places_out, n_outs, me_ref, *refs):
    pieces, outs, sems = refs[: -n_outs - 1], refs[-n_outs - 1 : -1], refs[-1]
    per, width = pieces[0].shape[0], pieces[0].shape[-1]
    heads = len(pieces) // places_out * per
    copies = []
    for index, piece in enumerate(pieces):
        for part in range(per):
            head = index // places_out * per + part
            place = (me_ref[1] ^ (index % places_out)) * heads + head
            columns = pl.ds(pl.multiple_of(place * width, width), width)
            for i, out in enumerate(outs):
                source = piece.at[part] if n_outs == 1 else piece.at[part, i]
                copies.append(
                    pltpu.make_async_copy(source, out.at[:, columns], sems.at[i, index, part])
                )
    for copy in copies:
        copy.start()
    for copy in copies:
        copy.wait()


def assemble(me, groups, n_outs):
    places_out = len(groups[0])
    pieces = [piece for group in groups for piece in group]
    per, share, width = pieces[0].shape[0], *pieces[0].shape[-2:]
    out = jax.ShapeDtypeStruct((share, len(pieces) * per * width), BF16)
    return pl.pallas_call(
        functools.partial(assemble_kernel, places_out, n_outs),
        out_shape=[out] * n_outs,
        in_specs=[SMEM] + [VMEM] * len(pieces),
        out_specs=[ANY] * n_outs,
        scratch_shapes=[pltpu.SemaphoreType.DMA((n_outs, len(pieces), per))],
        compiler_params=pltpu.CompilerParams(vmem_limit_bytes=4 * MIB),
    )(me, *pieces)


def swap(x):
    return lax.ppermute(x, "ctx", [(i, i ^ 1) for i in range(lax.axis_size("ctx"))])


def far(x, by):
    size = lax.axis_size("ctx")
    pairs = [(i, (i + (by if i % 2 == 0 else -by)) % size) for i in range(size)]
    return lax.ppermute(x, "ctx", pairs)


def after(x, *others):
    return lax.optimization_barrier((x, *others))[0] if others else x


def exchange(pieces):
    return [
        piece if k == 0 else lax.ppermute(piece, "head", [(i, i ^ k) for i in range(len(pieces))])
        for k, piece in enumerate(pieces)
    ]


def on_device(queries, keys, values, output_gradient, blocks, counts):
    tokens = queries.shape[0]
    cycle_blocks = lax.axis_size("ctx") * (tokens // BLOCK_TOKENS)
    places_out = lax.axis_size("head")
    me = jnp.stack([lax.axis_index("ctx"), lax.axis_index("head")])
    heads = keys.shape[1] // HEAD_SIZE

    rows = arrange(heads, queries, output_gradient)
    windows = []
    for own in pack(keys, values):
        if windows:
            own = after(own, windows[-1][AHEAD])
        ahead, behind, other = far(own, -REACH), far(own, REACH), swap(own)
        crossed = swap(ahead if windows else after(ahead, *rows[0]))
        windows.append([behind, crossed, own, other, ahead])
    dq_pieces, parts, sent = [], [], ()
    for (q_rows, o_rows), window in zip(rows, windows):
        outs = attention(cycle_blocks, places_out, (blocks, counts, me), q_rows, o_rows, window)
        pieces, outs = outs[:places_out], after(outs[places_out:], *sent)
        plain, near = far(outs[BEHIND], -REACH), swap(outs[CROSS])
        joined = (outs[AHEAD].astype(F32) + near.astype(F32)).astype(BF16)
        other = swap(outs[OTHER])
        dq_pieces.append(exchange(pieces))
        sent = (near, plain, other)
        parts += [outs[OWN], other, plain, far(joined, REACH)]
    (dqueries,) = assemble(me, dq_pieces, 1)
    dkv_pieces = exchange(sum_parts(me, parts, places_out))
    dkeys, dvalues = assemble(me, [dkv_pieces], 2)
    return dqueries, dkeys, dvalues


def solution(mesh):
    return jax.shard_map(
        on_device,
        mesh=mesh,
        in_specs=(
            P("ctx", "head"),
            P("ctx", "head"),
            P("ctx", "head"),
            P("ctx", "head"),
            P("ctx", None),
            P("ctx"),
        ),
        out_specs=(P(("ctx", "head"), None), P(("ctx", "head"), None), P(("ctx", "head"), None)),
        check_vma=False,
    )
```

time: 89.5 us -> 86.2 us (0.963)
  waiting for transfers between devices: 33.5 us -> 25.5 us
  starting transfers between devices: 32.1 us -> 35.7 us
  Pallas kernels: 20.8 us -> 22.1 us
    ppermute x16, waiting for transfers between devices: 28.9 us -> 16.1 us  [the longest x8 11.4 us: far(): return lax.ppermute(x, 'ctx', pairs)]
    ppermute x12 -> x9, waiting for transfers between devices: 4.61 us -> 9.31 us  [exchange(): lax.ppermute(piece, 'head', [(i, i ^ k) for i in range(len(pieces))])]
    ppermute x16, starting transfers between devices: 26.1 us -> 28.8 us  [the longest x8 17.7 us: far(): return lax.ppermute(x, 'ctx', pairs)]
    unnamed x8 -> x12, local copies, waits for them, and re-layouts: 0.61 us -> 2.46 us
    pallas_call x5 -> x7, Pallas kernels: 20.8 us -> 22.1 us  [the longest x2 15.1 us: attention(): pl.pallas_call(functools.partial(attention_kernel, cycle_blocks, places_o...]
    another operation x1 -> x0, local copies, waits for them, and re-layouts: 1.28 us -> none  [on_device(): own = jnp.stack([keys[:, columns], values[:, columns]])]
    ppermute x12 -> x9, starting transfers between devices: 5.92 us -> 6.81 us  [exchange(): lax.ppermute(piece, 'head', [(i, i ^ k) for i in range(len(pieces))])]
  transfers between devices with their start and end apart: 28 -> 25, of which waited for: 13 -> 11; matrix products, arithmetic and copies ran while one was open for 0% -> 0% of each run, Pallas kernels for 21% -> 22%
where the time goes in v3:
time: 86.2 us; the launch traced here: 86.9 us
  starting transfers between devices  35.7 us (41%)
  waiting for transfers between devices  25.5 us (30%)
  Pallas kernels  22.1 us (26%)
  local copies, waits for them, and re-layouts  2.46 us (3%)
  between operations  0.95 us (1%)
    ppermute x8, starting transfers between devices, far(): return lax.ppermute(x, 'ctx', pairs)  17.7 us
    pallas_call x2, Pallas kernels, attention(): pl.pallas_call(functools.partial(attention_kernel, cycle_blocks, places_o...  15.1 us
    ppermute x8, waiting for transfers between devices, far(): return lax.ppermute(x, 'ctx', pairs)  11.4 us
    ppermute x8, starting transfers between devices, swap(): lax.ppermute(x, 'ctx', [(i, i ^ 1) for i in range(lax.axis_size('ctx'))])  11.1 us
    ppermute x9, waiting for transfers between devices, exchange(): lax.ppermute(piece, 'head', [(i, i ^ k) for i in range(len(pieces))])  9.31 us
    ppermute x9, starting transfers between devices, exchange(): lax.ppermute(piece, 'head', [(i, i ^ k) for i in range(len(pieces))])  6.81 us
    ppermute x8, waiting for transfers between devices, swap(): lax.ppermute(x, 'ctx', [(i, i ^ 1) for i in range(lax.axis_size('ctx'))])  4.77 us
    pallas_call x2, Pallas kernels, assemble(): pl.pallas_call(functools.partial(assemble_kernel, places_out, n_outs), ou...  3.03 us
  transfers between devices with their start and end apart: 25, of which 11 were waited for; matrix products, arithmetic and copies ran while one was open for 0% of the time, Pallas kernels for 22%

profile of v3, /device:TPU:0, one launch (start us, length us, event | category | flops | bytes accessed | tf_op | source)
XLA Modules:
  0.0 86.9 jit_solution(5709908452244266862)
XLA Ops:
  0.6 1.9 %shard_map.86 = (bf16[2,512,128]{2,1,0:T(8,128)(2,1)}, bf16[2,512,128]{2,1,0:T(8,128)(2,1)}) custom-call(bf16[512,256]{1,0:T(8,128)(2,1)} %keys_hbm.1, bf16[512,256]{1,0:T(8,128)(2,1)} %values_hbm.1), custom_call_target="tpu_custom_call" | custom-call | tf_op jit(solution)/shard_map/pallas_call | solution.py:218
  2.6 5.1 %collective-permute-start.1 = (bf16[2,512,128]{2,1,0:T(8,128)(2,1)}, bf16[2,512,128]{2,1,0:T(8,128)(2,1)S(1)}, u32[]{:S(2)}, u32[]{:S(2)}) collective-permute-start(bf16[2,512,128]{2,1,0:T(8,128)(2,1)} %get-tuple-element.42.refs_7_), channel_id=1, source_target_pairs={{0,24},{4,12},{8,0},{12,20},{16,8},{20,28},{24,16},{28,4},{1,25},{... | collective-permute-start | bytes 786440 | tf_op jit(solution)/shard_map/ppermute | solution.py:294
  7.7 0.0 collective-permute-start
  7.7 1.7 %collective-permute-start.3 = (bf16[2,512,128]{2,1,0:T(8,128)(2,1)}, bf16[2,512,128]{2,1,0:T(8,128)(2,1)}, u32[]{:S(2)}, u32[]{:S(2)}) collective-permute-start(bf16[2,512,128]{2,1,0:T(8,128)(2,1)} %get-tuple-element.42.refs_7_), channel_id=1, source_target_pairs={{0,4},{4,0},{8,12},{12,8},{16,20},{20,16},{24,28},{28,24},{1,5},{5... | collective-permute-start | bytes 786440 | tf_op jit(solution)/shard_map/ppermute | solution.py:288
  9.4 1.2 %copy-done = bf16[512,1024]{1,0:T(8,128)(2,1)S(1)} copy-done((bf16[512,1024]{1,0:T(8,128)(2,1)S(1)}, bf16[512,1024]{1,0:T(8,128)(2,1)}, u32[]{:S(2)}) %copy-start) | copy-done | bytes 1048600
  10.6 1.2 %copy-done.1 = bf16[512,1024]{1,0:T(8,128)(2,1)S(1)} copy-done((bf16[512,1024]{1,0:T(8,128)(2,1)S(1)}, bf16[512,1024]{1,0:T(8,128)(2,1)}, u32[]{:S(2)}) %copy-start.1) | copy-done | bytes 1048600
  11.9 1.2 %shard_map.85 = (bf16[2048,128]{1,0:T(8,128)(2,1)S(1)}, bf16[2048,128]{1,0:T(8,128)(2,1)S(1)}, bf16[2048,128]{1,0:T(8,128)(2,1)S(1)}, bf16[2048,128]{1,0:T(8,128)(2,1)S(1)}) custom-call(bf16[512,1024]{1,0:T(8,128)(2,1)S(1)} %copy-done, bf16[512,1024]{1,0:T(8,128)(2,1)S(1)} %copy-done.1), custom_call_target="tpu_custom_call" | custom-call | bytes 8388608 | tf_op jit(solution)/shard_map/pallas_call | solution.py:189
  13.1 1.6 %collective-permute-done.1.refs_9_ = bf16[2,512,128]{2,1,0:T(8,128)(2,1)S(1)} collective-permute-done((bf16[2,512,128]{2,1,0:T(8,128)(2,1)}, bf16[2,512,128]{2,1,0:T(8,128)(2,1)S(1)}, u32[]{:S(2)}, u32[]{:S(2)}) %collective-permute-start.1) | collective-permute-done | bytes 262176 | tf_op jit(solution)/shard_map/ppermute | solution.py:294
  14.7 0.0 copy-done.2
  14.7 4.2 %collective-permute-start.8 = (bf16[2,512,128]{2,1,0:T(8,128)(2,1)S(1)}, bf16[2,512,128]{2,1,0:T(8,128)(2,1)S(1)}, u32[]{:S(2)}, u32[]{:S(2)}) collective-permute-start(bf16[2,512,128]{2,1,0:T(8,128)(2,1)S(1)} %copy-done.2), channel_id=1, source_target_pairs={{0,24},{4,12},{8,0},{12,20},{16,8},{20,28},{24,16},{28,4},{1,25},{... | collective-permute-start | bytes 786440 | tf_op jit(solution)/shard_map/ppermute | solution.py:294
  18.9 0.0 collective-permute-start.2
  18.9 0.1 pad_add_fusion.refs_2_.me_ref
  19.0 2.0 %collective-permute-start.10 = (bf16[2,512,128]{2,1,0:T(8,128)(2,1)S(1)}, bf16[2,512,128]{2,1,0:T(8,128)(2,1)S(1)}, u32[]{:S(2)}, u32[]{:S(2)}) collective-permute-start(bf16[2,512,128]{2,1,0:T(8,128)(2,1)S(1)} %copy-done.2), channel_id=1, source_target_pairs={{0,4},{4,0},{8,12},{12,8},{16,20},{20,16},{24,28},{28,24},{1,5},{5... | collective-permute-start | bytes 786440 | tf_op jit(solution)/shard_map/ppermute | solution.py:288
  21.0 0.2 collective-permute-done.refs_5_
  21.2 1.5 %collective-permute-start.7 = (bf16[2,512,128]{2,1,0:T(8,128)(2,1)S(1)}, bf16[2,512,128]{2,1,0:T(8,128)(2,1)S(1)}, u32[]{:S(2)}, u32[]{:S(2)}) collective-permute-start(bf16[2,512,128]{2,1,0:T(8,128)(2,1)S(1)} %copy-done.2), channel_id=1, source_target_pairs={{0,8},{4,28},{8,16},{12,4},{16,24},{20,12},{24,0},{28,20},{1,9},{5... | collective-permute-start | bytes 786440 | tf_op jit(solution)/shard_map/ppermute | solution.py:294
  22.7 3.7 %collective-permute-done.8.refs_9_ = bf16[2,512,128]{2,1,0:T(8,128)(2,1)S(1)} collective-permute-done((bf16[2,512,128]{2,1,0:T(8,128)(2,1)S(1)}, bf16[2,512,128]{2,1,0:T(8,128)(2,1)S(1)}, u32[]{:S(2)}, u32[]{:S(2)}) %collective-permute-start.8) | collective-permute-done | bytes 262176 | tf_op jit(solution)/shard_map/ppermute | solution.py:294
  26.4 2.9 %collective-permute-start.9 = (bf16[2,512,128]{2,1,0:T(8,128)(2,1)S(1)}, bf16[2,512,128]{2,1,0:T(8,128)(2,1)S(1)}, u32[]{:S(2)}, u32[]{:S(2)}) collective-permute-start(bf16[2,512,128]{2,1,0:T(8,128)(2,1)S(1)} %collective-permute-done.8.refs_9_), channel_id=1, source_target_pairs={{0,4},{4,0},{8,12},{12,8},{16,20},{20,16},{24,28},{28,24},{1,5},{5... | collective-permute-start | bytes 786440 | tf_op jit(solution)/shard_map/ppermute | solution.py:288
  29.3 0.0 collective-permute-done.3.refs_8_
  29.3 0.0 collective-permute-done.2.refs_6_
  29.3 0.0 copy-done.3
  29.3 7.9 %shard_map.87 = (bf16[1,128,512]{2,1,0:T(8,128)(2,1)S(1)}, bf16[1,128,512]{2,1,0:T(8,128)(2,1)S(1)}, bf16[1,128,512]{2,1,0:T(8,128)(2,1)S(1)}, bf16[1,128,512]{2...) custom-call(s32[4,8]{1,0:T(4,128)S(1)} %copy-done.4, ...), custom_call_target="tpu_custom_call" | custom-call | flops 10000000000 | bytes 20000000 | tf_op jit(solution)/shard_map/pallas_call | solution.py:138
  37.3 1.2 %collective-permute-start.14 = (bf16[2,512,128]{2,1,0:T(8,128)(2,1)S(1)}, bf16[2,512,128]{2,1,0:T(8,128)(2,1)S(1)}, u32[]{:S(2)}, u32[]{:S(2)}) collective-permute-start(bf16[2,512,128]{2,1,0:T(8,128)(2,1)S(1)} %get-tuple-element.57), channel_id=1, source_target_pairs={{0,4},{4,0},{8,12},{12,8},{16,20},{20,16},{24,28},{28,24},{1,5},{5... | collective-permute-start | bytes 786440 | tf_op jit(solution)/shard_map/ppermute | solution.py:288
  38.4 4.8 %collective-permute-start.15 = (bf16[2,512,128]{2,1,0:T(8,128)(2,1)S(1)}, bf16[2,512,128]{2,1,0:T(8,128)(2,1)S(1)}, u32[]{:S(2)}, u32[]{:S(2)}) collective-permute-start(bf16[2,512,128]{2,1,0:T(8,128)(2,1)S(1)} %get-tuple-element.58), channel_id=1, source_target_pairs={{0,24},{4,12},{8,0},{12,20},{16,8},{20,28},{24,16},{28,4},{1,25},{... | collective-permute-start | bytes 786440 | tf_op jit(solution)/shard_map/ppermute | solution.py:294
  43.2 0.0 collective-permute-done.10.refs_8_
  43.2 0.0 collective-permute-start.16
  43.2 0.0 collective-permute-done.7.refs_5_
  43.2 0.0 collective-permute-done.9.refs_6_
  43.2 7.2 %shard_map.88 = (bf16[1,128,512]{2,1,0:T(8,128)(2,1)S(1)}, bf16[1,128,512]{2,1,0:T(8,128)(2,1)S(1)}, bf16[1,128,512]{2,1,0:T(8,128)(2,1)S(1)}, bf16[1,128,512]{2...) custom-call(s32[4,8]{1,0:T(4,128)S(1)} %copy-done.4, ...), custom_call_target="tpu_custom_call" | custom-call | flops 10000000000 | bytes 20000000 | tf_op jit(solution)/shard_map/pallas_call | solution.py:138
  50.4 0.0 collective-permute-done.14.refs_1_
  50.4 0.0 collective-permute-done.15.refs_2_
  50.5 0.0 collective-permute-done.16
  50.5 3.1 %collective-permute-start.20 = (bf16[2,512,128]{2,1,0:T(8,128)(2,1)S(1)}, bf16[2,512,128]{2,1,0:T(8,128)(2,1)S(1)}, u32[]{:S(2)}, u32[]{:S(2)}) collective-permute-start(bf16[2,512,128]{2,1,0:T(8,128)(2,1)S(1)} %get-tuple-element.70), channel_id=1, source_target_pairs={{0,4},{4,0},{8,12},{12,8},{16,20},{20,16},{24,28},{28,24},{1,5},{5... | collective-permute-start | bytes 786440 | tf_op jit(solution)/shard_map/ppermute | solution.py:288
  53.6 0.1 collective-permute-start.18
  53.7 1.4 %collective-permute-start.19 = (bf16[2,512,128]{2,1,0:T(8,128)(2,1)S(1)}, bf16[2,512,128]{2,1,0:T(8,128)(2,1)S(1)}, u32[]{:S(2)}, u32[]{:S(2)}) collective-permute-start(bf16[2,512,128]{2,1,0:T(8,128)(2,1)S(1)} %get-tuple-element.68), channel_id=1, source_target_pairs={{0,24},{4,12},{8,0},{12,20},{16,8},{20,28},{24,16},{28,4},{1,25},{... | collective-permute-start | bytes 786440 | tf_op jit(solution)/shard_map/ppermute | solution.py:294
  55.1 0.1 add_convert_fusion.1
  55.2 0.6 collective-permute-start.17
  55.8 2.2 %collective-permute-done.20 = bf16[2,512,128]{2,1,0:T(8,128)(2,1)S(1)} collective-permute-done((bf16[2,512,128]{2,1,0:T(8,128)(2,1)S(1)}, bf16[2,512,128]{2,1,0:T(8,128)(2,1)S(1)}, u32[]{:S(2)}, u32[]{:S(2)}) %collective-permute-start.20) | collective-permute-done | bytes 262176 | tf_op jit(solution)/shard_map/ppermute | solution.py:288
  58.0 0.1 add_convert_fusion
  58.1 0.1 collective-permute-start.21
  58.2 0.0 collective-permute-start.4
  58.2 2.6 %collective-permute-done.18.refs_5_ = bf16[2,512,128]{2,1,0:T(8,128)(2,1)S(1)} collective-permute-done((bf16[2,512,128]{2,1,0:T(8,128)(2,1)S(1)}, bf16[2,512,128]{2,1,0:T(8,128)(2,1)S(1)}, u32[]{:S(2)}, u32[]{:S(2)}) %collective-permute-start.18) | collective-permute-done | bytes 262176 | tf_op jit(solution)/shard_map/ppermute | solution.py:288
  60.8 1.5 %collective-permute-start.5 = (bf16[1,128,512]{2,1,0:T(8,128)(2,1)S(1)}, bf16[1,128,512]{2,1,0:T(8,128)(2,1)S(1)}, u32[]{:S(2)}, u32[]{:S(2)}) collective-permute-start(bf16[1,128,512]{2,1,0:T(8,128)(2,1)S(1)} %get-tuple-element.46), channel_id=1, source_target_pairs={{0,2},{1,3},{2,0},{3,1},{4,6},{5,7},{6,4},{7,5},{8,10},{9,11},{10,... | collective-permute-start | bytes 393224 | tf_op jit(solution)/shard_map/ppermute | solution.py:303
  62.3 5.9 %collective-permute-done.19.refs_6_ = bf16[2,512,128]{2,1,0:T(8,128)(2,1)S(1)} collective-permute-done((bf16[2,512,128]{2,1,0:T(8,128)(2,1)S(1)}, bf16[2,512,128]{2,1,0:T(8,128)(2,1)S(1)}, u32[]{:S(2)}, u32[]{:S(2)}) %collective-permute-start.19) | collective-permute-done | bytes 262176 | tf_op jit(solution)/shard_map/ppermute | solution.py:294
  68.2 0.0 collective-permute-start.6
  68.2 0.0 collective-permute-done.17.refs_3_
  68.2 1.6 %collective-permute-start.11 = (bf16[1,128,512]{2,1,0:T(8,128)(2,1)S(1)}, bf16[1,128,512]{2,1,0:T(8,128)(2,1)S(1)}, u32[]{:S(2)}, u32[]{:S(2)}) collective-permute-start(bf16[1,128,512]{2,1,0:T(8,128)(2,1)S(1)} %get-tuple-element.53), channel_id=1, source_target_pairs={{0,1},{1,0},{2,3},{3,2},{4,5},{5,4},{6,7},{7,6},{8,9},{9,8},{10,11... | collective-permute-start | bytes 393224 | tf_op jit(solution)/shard_map/ppermute | solution.py:303
  69.8 0.0 collective-permute-done.21.refs_7_
  69.8 0.5 collective-permute-start.12
  70.4 0.8 shard_map.90
  71.2 0.0 collective-permute-done.4.refs_1_
  71.2 0.9 %collective-permute-start.13 = (bf16[1,128,512]{2,1,0:T(8,128)(2,1)S(1)}, bf16[1,128,512]{2,1,0:T(8,128)(2,1)S(1)}, u32[]{:S(2)}, u32[]{:S(2)}) collective-permute-start(bf16[1,128,512]{2,1,0:T(8,128)(2,1)S(1)} %get-tuple-element.55), channel_id=1, source_target_pairs={{0,3},{1,2},{2,1},{3,0},{4,7},{5,6},{6,5},{7,4},{8,11},{9,10},{10,... | collective-permute-start | bytes 393224 | tf_op jit(solution)/shard_map/ppermute | solution.py:303
  72.1 0.0 collective-permute-done.5.refs_2_
  72.2 0.7 collective-permute-start.22
  72.9 1.1 %collective-permute-done.6.refs_3_ = bf16[1,128,512]{2,1,0:T(8,128)(2,1)S(1)} collective-permute-done((bf16[1,128,512]{2,1,0:T(8,128)(2,1)S(1)}, bf16[1,128,512]{2,1,0:T(8,128)(2,1)S(1)}, u32[]{:S(2)}, u32[]{:S(2)}) %collective-permute-start.6) | collective-permute-done | bytes 131104 | tf_op jit(solution)/shard_map/ppermute | solution.py:303
  74.0 1.2 %collective-permute-start.23 = (bf16[2,2,128,128]{3,2,1,0:T(8,128)(2,1)S(1)}, bf16[2,2,128,128]{3,2,1,0:T(8,128)(2,1)S(1)}, u32[]{:S(2)}, u32[]{:S(2)}) collective-permute-start(bf16[2,2,128,128]{3,2,1,0:T(8,128)(2,1)S(1)} %get-tuple-element.73), channel_id=1, source_target_pairs={{0,2},{1,3},{2,0},{3,1},{4,6},{5,7},{6,4},{7,5},{8,10},{9,11},{10,... | collective-permute-start | bytes 393224 | tf_op jit(solution)/shard_map/ppermute | solution.py:303
  75.2 0.0 collective-permute-done.11.refs_5_
  75.2 0.2 collective-permute-start.24
  75.5 1.4 %collective-permute-done.12.refs_6_ = bf16[1,128,512]{2,1,0:T(8,128)(2,1)S(1)} collective-permute-done((bf16[1,128,512]{2,1,0:T(8,128)(2,1)S(1)}, bf16[1,128,512]{2,1,0:T(8,128)(2,1)S(1)}, u32[]{:S(2)}, u32[]{:S(2)}) %collective-permute-start.12) | collective-permute-done | bytes 131104 | tf_op jit(solution)/shard_map/ppermute | solution.py:303
  76.9 2.7 %collective-permute-done.13.refs_7_ = bf16[1,128,512]{2,1,0:T(8,128)(2,1)S(1)} collective-permute-done((bf16[1,128,512]{2,1,0:T(8,128)(2,1)S(1)}, bf16[1,128,512]{2,1,0:T(8,128)(2,1)S(1)}, u32[]{:S(2)}, u32[]{:S(2)}) %collective-permute-start.13) | collective-permute-done | bytes 131104 | tf_op jit(solution)/shard_map/ppermute | solution.py:303
  79.6 1.6 %shard_map.89 = bf16[128,4096]{1,0:T(8,128)(2,1)} custom-call(s32[2]{0:T(128)S(1)} %pad_add_fusion.refs_2_.me_ref, bf16[1,128,512]{2,1,0:T(8,128)(2,1)S(1)} %get-tuple-element.44.refs_0_, bf16[1,128,512]{2,1,0:T(8,128)(2,1)S(1)} %collective-permute-done.4.refs_1_, bf16[1,128,512]{2,1,0:T(8,128)(2,1)S(1)} %collective-permute-done.5.refs_2_, ...), custom_call_target="tpu_custom_call" | custom-call | tf_op jit(solution)/shard_map/pallas_call | solution.py:277
  81.2 0.0 collective-permute-done.22.refs_1_
  81.2 1.3 %collective-permute-done.23.refs_2_ = bf16[2,2,128,128]{3,2,1,0:T(8,128)(2,1)S(1)} collective-permute-done((bf16[2,2,128,128]{3,2,1,0:T(8,128)(2,1)S(1)}, bf16[2,2,128,128]{3,2,1,0:T(8,128)(2,1)S(1)}, u32[]{:S(2)}, u32[]{:S(2)}) %collective-permute-start.23) | collective-permute-done | bytes 131104 | tf_op jit(solution)/shard_map/ppermute | solution.py:303
  82.5 2.7 %collective-permute-done.24.refs_3_ = bf16[2,2,128,128]{3,2,1,0:T(8,128)(2,1)S(1)} collective-permute-done((bf16[2,2,128,128]{3,2,1,0:T(8,128)(2,1)S(1)}, bf16[2,2,128,128]{3,2,1,0:T(8,128)(2,1)S(1)}, u32[]{:S(2)}, u32[]{:S(2)}) %collective-permute-start.24) | collective-permute-done | bytes 131104 | tf_op jit(solution)/shard_map/ppermute | solution.py:303
  85.2 1.5 %shard_map.91 = (bf16[128,1024]{1,0:T(8,128)(2,1)}, bf16[128,1024]{1,0:T(8,128)(2,1)}) custom-call(s32[2]{0:T(128)S(1)} %pad_add_fusion.refs_2_.me_ref, bf16[2,2,128,128]{3,2,1,0:T(8,128)(2,1)S(1)} %get-tuple-element.71.refs_0_, bf16[2,2,128,128]{3,2,1,0:T(8,128)(2,1)S(1)} %collective-permute-done.22.refs_1_, ...), custom_call_target="tpu_custom_call" | custom-call | tf_op jit(solution)/shard_map/pallas_call | solution.py:277
  (8 shorter events, 0.0 us)
Async XLA Ops:
  2.6 12.1 %collective-permute-start.1 = (bf16[2,512,128]{2,1,0:T(8,128)(2,1)}, bf16[2,512,128]{2,1,0:T(8,128)(2,1)S(1)}, u32[]{:S(2)}, u32[]{:S(2)}) collective-permute-start(bf16[2,512,128]{2,1,0:T(8,128)(2,1)} %get-tuple-element.42.refs_7_), channel_id=1, source_target_pairs={{0,24},{4,12},{8,0},{12,20},{16,8},{20,28},{24,16},{28,4},{1,25},{... | collective-permute-start | bytes 786440 | tf_op jit(solution)/shard_map/ppermute | solution.py:294
  7.7 13.5 %collective-permute-start = (bf16[2,512,128]{2,1,0:T(8,128)(2,1)}, bf16[2,512,128]{2,1,0:T(8,128)(2,1)S(1)}, u32[]{:S(2)}, u32[]{:S(2)}) collective-permute-start(bf16[2,512,128]{2,1,0:T(8,128)(2,1)} %get-tuple-element.42.refs_7_), channel_id=1, source_target_pairs={{0,8},{4,28},{8,16},{12,4},{16,24},{20,12},{24,0},{28,20},{1,9},{5... | collective-permute-start | bytes 786440 | tf_op jit(solution)/shard_map/ppermute | solution.py:294
  7.7 21.7 %collective-permute-start.3 = (bf16[2,512,128]{2,1,0:T(8,128)(2,1)}, bf16[2,512,128]{2,1,0:T(8,128)(2,1)}, u32[]{:S(2)}, u32[]{:S(2)}) collective-permute-start(bf16[2,512,128]{2,1,0:T(8,128)(2,1)} %get-tuple-element.42.refs_7_), channel_id=1, source_target_pairs={{0,4},{4,0},{8,12},{12,8},{16,20},{20,16},{24,28},{28,24},{1,5},{5... | collective-permute-start | bytes 786440 | tf_op jit(solution)/shard_map/ppermute | solution.py:288
  9.4 1.2 %copy-start = (bf16[512,1024]{1,0:T(8,128)(2,1)S(1)}, bf16[512,1024]{1,0:T(8,128)(2,1)}, u32[]{:S(2)}) copy-start(bf16[512,1024]{1,0:T(8,128)(2,1)} %queries_hbm.1) | copy-start | bytes 3145732
  10.6 1.2 %copy-start.1 = (bf16[512,1024]{1,0:T(8,128)(2,1)S(1)}, bf16[512,1024]{1,0:T(8,128)(2,1)}, u32[]{:S(2)}) copy-start(bf16[512,1024]{1,0:T(8,128)(2,1)} %outgrad_hbm.1) | copy-start | bytes 3145732
  11.8 2.8 %copy-start.2 = (bf16[2,512,128]{2,1,0:T(8,128)(2,1)S(1)}, bf16[2,512,128]{2,1,0:T(8,128)(2,1)}, u32[]{:S(2)}) copy-start(bf16[2,512,128]{2,1,0:T(8,128)(2,1)} %get-tuple-element.51.refs_7_) | copy-start | bytes 786436
  11.9 17.5 %copy-start.3 = (bf16[2,512,128]{2,1,0:T(8,128)(2,1)S(1)}, bf16[2,512,128]{2,1,0:T(8,128)(2,1)}, u32[]{:S(2)}) copy-start(bf16[2,512,128]{2,1,0:T(8,128)(2,1)} %get-tuple-element.42.refs_7_) | copy-start | bytes 786436
  14.7 11.7 %collective-permute-start.8 = (bf16[2,512,128]{2,1,0:T(8,128)(2,1)S(1)}, bf16[2,512,128]{2,1,0:T(8,128)(2,1)S(1)}, u32[]{:S(2)}, u32[]{:S(2)}) collective-permute-start(bf16[2,512,128]{2,1,0:T(8,128)(2,1)S(1)} %copy-done.2), channel_id=1, source_target_pairs={{0,24},{4,12},{8,0},{12,20},{16,8},{20,28},{24,16},{28,4},{1,25},{... | collective-permute-start | bytes 786440 | tf_op jit(solution)/shard_map/ppermute | solution.py:294
  18.9 10.4 %collective-permute-start.2 = (bf16[2,512,128]{2,1,0:T(8,128)(2,1)S(1)}, bf16[2,512,128]{2,1,0:T(8,128)(2,1)}, u32[]{:S(2)}, u32[]{:S(2)}) collective-permute-start(bf16[2,512,128]{2,1,0:T(8,128)(2,1)S(1)} %collective-permute-done.1.refs_9_), channel_id=1, source_target_pairs={{0,4},{4,0},{8,12},{12,8},{16,20},{20,16},{24,28},{28,24},{1,5},{5... | collective-permute-start | bytes 786440 | tf_op jit(solution)/shard_map/ppermute | solution.py:288
  18.9 10.5 %copy-start.4 = (s32[4,8]{1,0:T(4,128)S(1)}, s32[4,8]{1,0:T(4,128)}, u32[]{:S(2)}) copy-start(s32[4,8]{1,0:T(4,128)} %refs_0_.3) | copy-start | bytes 388
  18.9 10.5 %copy-start.5 = (s32[4]{0:T(128)S(1)}, s32[4]{0:T(128)}, u32[]{:S(2)}) copy-start(s32[4]{0:T(128)} %refs_1_.3) | copy-start | bytes 52
  19.0 24.3 %collective-permute-start.10 = (bf16[2,512,128]{2,1,0:T(8,128)(2,1)S(1)}, bf16[2,512,128]{2,1,0:T(8,128)(2,1)S(1)}, u32[]{:S(2)}, u32[]{:S(2)}) collective-permute-start(bf16[2,512,128]{2,1,0:T(8,128)(2,1)S(1)} %copy-done.2), channel_id=1, source_target_pairs={{0,4},{4,0},{8,12},{12,8},{16,20},{20,16},{24,28},{28,24},{1,5},{5... | collective-permute-start | bytes 786440 | tf_op jit(solution)/shard_map/ppermute | solution.py:288
  21.2 22.1 %collective-permute-start.7 = (bf16[2,512,128]{2,1,0:T(8,128)(2,1)S(1)}, bf16[2,512,128]{2,1,0:T(8,128)(2,1)S(1)}, u32[]{:S(2)}, u32[]{:S(2)}) collective-permute-start(bf16[2,512,128]{2,1,0:T(8,128)(2,1)S(1)} %copy-done.2), channel_id=1, source_target_pairs={{0,8},{4,28},{8,16},{12,4},{16,24},{20,12},{24,0},{28,20},{1,9},{5... | collective-permute-start | bytes 786440 | tf_op jit(solution)/shard_map/ppermute | solution.py:294
  26.4 16.9 %collective-permute-start.9 = (bf16[2,512,128]{2,1,0:T(8,128)(2,1)S(1)}, bf16[2,512,128]{2,1,0:T(8,128)(2,1)S(1)}, u32[]{:S(2)}, u32[]{:S(2)}) collective-permute-start(bf16[2,512,128]{2,1,0:T(8,128)(2,1)S(1)} %collective-permute-done.8.refs_9_), channel_id=1, source_target_pairs={{0,4},{4,0},{8,12},{12,8},{16,20},{20,16},{24,28},{28,24},{1,5},{5... | collective-permute-start | bytes 786440 | tf_op jit(solution)/shard_map/ppermute | solution.py:288
  37.3 13.2 %collective-permute-start.14 = (bf16[2,512,128]{2,1,0:T(8,128)(2,1)S(1)}, bf16[2,512,128]{2,1,0:T(8,128)(2,1)S(1)}, u32[]{:S(2)}, u32[]{:S(2)}) collective-permute-start(bf16[2,512,128]{2,1,0:T(8,128)(2,1)S(1)} %get-tuple-element.57), channel_id=1, source_target_pairs={{0,4},{4,0},{8,12},{12,8},{16,20},{20,16},{24,28},{28,24},{1,5},{5... | collective-permute-start | bytes 786440 | tf_op jit(solution)/shard_map/ppermute | solution.py:288
  38.4 12.0 %collective-permute-start.15 = (bf16[2,512,128]{2,1,0:T(8,128)(2,1)S(1)}, bf16[2,512,128]{2,1,0:T(8,128)(2,1)S(1)}, u32[]{:S(2)}, u32[]{:S(2)}) collective-permute-start(bf16[2,512,128]{2,1,0:T(8,128)(2,1)S(1)} %get-tuple-element.58), channel_id=1, source_target_pairs={{0,24},{4,12},{8,0},{12,20},{16,8},{20,28},{24,16},{28,4},{1,25},{... | collective-permute-start | bytes 786440 | tf_op jit(solution)/shard_map/ppermute | solution.py:294
  43.2 7.2 %collective-permute-start.16 = (bf16[2,512,128]{2,1,0:T(8,128)(2,1)S(1)}, bf16[2,512,128]{2,1,0:T(8,128)(2,1)S(1)}, u32[]{:S(2)}, u32[]{:S(2)}) collective-permute-start(bf16[2,512,128]{2,1,0:T(8,128)(2,1)S(1)} %get-tuple-element.60), channel_id=1, source_target_pairs={{0,4},{4,0},{8,12},{12,8},{16,20},{20,16},{24,28},{28,24},{1,5},{5... | collective-permute-start | bytes 786440 | tf_op jit(solution)/shard_map/ppermute | solution.py:288
  50.5 7.5 %collective-permute-start.20 = (bf16[2,512,128]{2,1,0:T(8,128)(2,1)S(1)}, bf16[2,512,128]{2,1,0:T(8,128)(2,1)S(1)}, u32[]{:S(2)}, u32[]{:S(2)}) collective-permute-start(bf16[2,512,128]{2,1,0:T(8,128)(2,1)S(1)} %get-tuple-element.70), channel_id=1, source_target_pairs={{0,4},{4,0},{8,12},{12,8},{16,20},{20,16},{24,28},{28,24},{1,5},{5... | collective-permute-start | bytes 786440 | tf_op jit(solution)/shard_map/ppermute | solution.py:288
  53.6 7.2 %collective-permute-start.18 = (bf16[2,512,128]{2,1,0:T(8,128)(2,1)S(1)}, bf16[2,512,128]{2,1,0:T(8,128)(2,1)S(1)}, u32[]{:S(2)}, u32[]{:S(2)}) collective-permute-start(bf16[2,512,128]{2,1,0:T(8,128)(2,1)S(1)} %get-tuple-element.67), channel_id=1, source_target_pairs={{0,4},{4,0},{8,12},{12,8},{16,20},{20,16},{24,28},{28,24},{1,5},{5... | collective-permute-start | bytes 786440 | tf_op jit(solution)/shard_map/ppermute | solution.py:288
  53.7 14.5 %collective-permute-start.19 = (bf16[2,512,128]{2,1,0:T(8,128)(2,1)S(1)}, bf16[2,512,128]{2,1,0:T(8,128)(2,1)S(1)}, u32[]{:S(2)}, u32[]{:S(2)}) collective-permute-start(bf16[2,512,128]{2,1,0:T(8,128)(2,1)S(1)} %get-tuple-element.68), channel_id=1, source_target_pairs={{0,24},{4,12},{8,0},{12,20},{16,8},{20,28},{24,16},{28,4},{1,25},{... | collective-permute-start | bytes 786440 | tf_op jit(solution)/shard_map/ppermute | solution.py:294
  55.2 13.0 %collective-permute-start.17 = (bf16[2,512,128]{2,1,0:T(8,128)(2,1)S(1)}, bf16[2,512,128]{2,1,0:T(8,128)(2,1)S(1)}, u32[]{:S(2)}, u32[]{:S(2)}) collective-permute-start(bf16[2,512,128]{2,1,0:T(8,128)(2,1)S(1)} %add_convert_fusion.1), channel_id=1, source_target_pairs={{0,8},{4,28},{8,16},{12,4},{16,24},{20,12},{24,0},{28,20},{1,9},{5... | collective-permute-start | bytes 786440 | tf_op jit(solution)/shard_map/ppermute | solution.py:294
  58.1 11.8 %collective-permute-start.21 = (bf16[2,512,128]{2,1,0:T(8,128)(2,1)S(1)}, bf16[2,512,128]{2,1,0:T(8,128)(2,1)S(1)}, u32[]{:S(2)}, u32[]{:S(2)}) collective-permute-start(bf16[2,512,128]{2,1,0:T(8,128)(2,1)S(1)} %add_convert_fusion), channel_id=1, source_target_pairs={{0,8},{4,28},{8,16},{12,4},{16,24},{20,12},{24,0},{28,20},{1,9},{5... | collective-permute-start | bytes 786440 | tf_op jit(solution)/shard_map/ppermute | solution.py:294
  58.2 13.0 %collective-permute-start.4 = (bf16[1,128,512]{2,1,0:T(8,128)(2,1)S(1)}, bf16[1,128,512]{2,1,0:T(8,128)(2,1)S(1)}, u32[]{:S(2)}, u32[]{:S(2)}) collective-permute-start(bf16[1,128,512]{2,1,0:T(8,128)(2,1)S(1)} %get-tuple-element.45), channel_id=1, source_target_pairs={{0,1},{1,0},{2,3},{3,2},{4,5},{5,4},{6,7},{7,6},{8,9},{9,8},{10,11... | collective-permute-start | bytes 393224 | tf_op jit(solution)/shard_map/ppermute | solution.py:303
  60.8 11.3 %collective-permute-start.5 = (bf16[1,128,512]{2,1,0:T(8,128)(2,1)S(1)}, bf16[1,128,512]{2,1,0:T(8,128)(2,1)S(1)}, u32[]{:S(2)}, u32[]{:S(2)}) collective-permute-start(bf16[1,128,512]{2,1,0:T(8,128)(2,1)S(1)} %get-tuple-element.46), channel_id=1, source_target_pairs={{0,2},{1,3},{2,0},{3,1},{4,6},{5,7},{6,4},{7,5},{8,10},{9,11},{10,... | collective-permute-start | bytes 393224 | tf_op jit(solution)/shard_map/ppermute | solution.py:303
  68.2 5.8 %collective-permute-start.6 = (bf16[1,128,512]{2,1,0:T(8,128)(2,1)S(1)}, bf16[1,128,512]{2,1,0:T(8,128)(2,1)S(1)}, u32[]{:S(2)}, u32[]{:S(2)}) collective-permute-start(bf16[1,128,512]{2,1,0:T(8,128)(2,1)S(1)} %get-tuple-element.47), channel_id=1, source_target_pairs={{0,3},{1,2},{2,1},{3,0},{4,7},{5,6},{6,5},{7,4},{8,11},{9,10},{10,... | collective-permute-start | bytes 393224 | tf_op jit(solution)/shard_map/ppermute | solution.py:303
  68.2 7.0 %collective-permute-start.11 = (bf16[1,128,512]{2,1,0:T(8,128)(2,1)S(1)}, bf16[1,128,512]{2,1,0:T(8,128)(2,1)S(1)}, u32[]{:S(2)}, u32[]{:S(2)}) collective-permute-start(bf16[1,128,512]{2,1,0:T(8,128)(2,1)S(1)} %get-tuple-element.53), channel_id=1, source_target_pairs={{0,1},{1,0},{2,3},{3,2},{4,5},{5,4},{6,7},{7,6},{8,9},{9,8},{10,11... | collective-permute-start | bytes 393224 | tf_op jit(solution)/shard_map/ppermute | solution.py:303
  69.8 7.0 %collective-permute-start.12 = (bf16[1,128,512]{2,1,0:T(8,128)(2,1)S(1)}, bf16[1,128,512]{2,1,0:T(8,128)(2,1)S(1)}, u32[]{:S(2)}, u32[]{:S(2)}) collective-permute-start(bf16[1,128,512]{2,1,0:T(8,128)(2,1)S(1)} %get-tuple-element.54), channel_id=1, source_target_pairs={{0,2},{1,3},{2,0},{3,1},{4,6},{5,7},{6,4},{7,5},{8,10},{9,11},{10,... | collective-permute-start | bytes 393224 | tf_op jit(solution)/shard_map/ppermute | solution.py:303
  71.2 8.4 %collective-permute-start.13 = (bf16[1,128,512]{2,1,0:T(8,128)(2,1)S(1)}, bf16[1,128,512]{2,1,0:T(8,128)(2,1)S(1)}, u32[]{:S(2)}, u32[]{:S(2)}) collective-permute-start(bf16[1,128,512]{2,1,0:T(8,128)(2,1)S(1)} %get-tuple-element.55), channel_id=1, source_target_pairs={{0,3},{1,2},{2,1},{3,0},{4,7},{5,6},{6,5},{7,4},{8,11},{9,10},{10,... | collective-permute-start | bytes 393224 | tf_op jit(solution)/shard_map/ppermute | solution.py:303
  72.2 9.0 %collective-permute-start.22 = (bf16[2,2,128,128]{3,2,1,0:T(8,128)(2,1)S(1)}, bf16[2,2,128,128]{3,2,1,0:T(8,128)(2,1)S(1)}, u32[]{:S(2)}, u32[]{:S(2)}) collective-permute-start(bf16[2,2,128,128]{3,2,1,0:T(8,128)(2,1)S(1)} %get-tuple-element.72), channel_id=1, source_target_pairs={{0,1},{1,0},{2,3},{3,2},{4,5},{5,4},{6,7},{7,6},{8,9},{9,8},{10,11... | collective-permute-start | bytes 393224 | tf_op jit(solution)/shard_map/ppermute | solution.py:303
  74.0 8.5 %collective-permute-start.23 = (bf16[2,2,128,128]{3,2,1,0:T(8,128)(2,1)S(1)}, bf16[2,2,128,128]{3,2,1,0:T(8,128)(2,1)S(1)}, u32[]{:S(2)}, u32[]{:S(2)}) collective-permute-start(bf16[2,2,128,128]{3,2,1,0:T(8,128)(2,1)S(1)} %get-tuple-element.73), channel_id=1, source_target_pairs={{0,2},{1,3},{2,0},{3,1},{4,6},{5,7},{6,4},{7,5},{8,10},{9,11},{10,... | collective-permute-start | bytes 393224 | tf_op jit(solution)/shard_map/ppermute | solution.py:303
  75.2 10.0 %collective-permute-start.24 = (bf16[2,2,128,128]{3,2,1,0:T(8,128)(2,1)S(1)}, bf16[2,2,128,128]{3,2,1,0:T(8,128)(2,1)S(1)}, u32[]{:S(2)}, u32[]{:S(2)}) collective-permute-start(bf16[2,2,128,128]{3,2,1,0:T(8,128)(2,1)S(1)} %get-tuple-element.74), channel_id=1, source_target_pairs={{0,3},{1,2},{2,1},{3,0},{4,7},{5,6},{6,5},{7,4},{8,11},{9,10},{10,... | collective-permute-start | bytes 393224 | tf_op jit(solution)/shard_map/ppermute | solution.py:303
